TPU v7x, 32 devices: a whole 2x2x4 slice. The times are simulated.
32 devices in a mesh: replica: 4 (over z), shard: 8 (over y, x, core).
Axes of the slice: x: 2, y: 2, z: 4, core: 2. Of those that a mesh axis runs over, the one named last changes fastest.
Arguments:
- tokens: bfloat16 [2, 32, 512, 768], P(None, ('replica', 'shard')), may hold values from -6 to 6
- cotangent: bfloat16 [2, 32, 512, 768], P(None, ('replica', 'shard')), may hold values from -6 to 6
- lengths: int32 [64], replicated, may hold values from 128 to 512, as said below
- dealing: int32 [64], replicated, may hold values from 0 to 63, each once
- in_gain: float32 [2, 768], replicated, may hold values from 0.5 to 1.5
- w_in: bfloat16 [2, 768, 3352], P(None, 'shard'), may hold values from -0.21875 to 0.21875
- conv_w: float32 [2, 4, 1792], replicated, may hold values from -3 to 3
- conv_b: float32 [2, 1792], replicated, may hold values from -3 to 3
- dt_bias: float32 [2, 24], replicated, may hold values from -6.9 to -2.3
- a_log: float32 [2, 24], replicated, may hold values from 0 to 2.77
- d_skip: float32 [2, 24], replicated, may hold values from 0.1 to 1.9
- out_gain: float32 [2, 1536], replicated, may hold values from 0.5 to 1.5
- w_out: bfloat16 [2, 1536, 768], P(None, 'shard'), may hold values from -0.15625 to 0.15625
Outputs:
- outputs: bfloat16 [2, 32, 512, 768], P(None, ('replica', 'shard'))
- grad_tokens: float32 [2, 32, 512, 768], P(None, ('replica', 'shard'))
- grad_in_gain: float32 [2, 768], replicated
- grad_w_in: float32 [2, 768, 3352], P(None, 'shard')
- grad_conv_w: float32 [2, 4, 1792], replicated
- grad_conv_b: float32 [2, 1792], replicated
- grad_dt_bias: float32 [2, 24], replicated
- grad_a_log: float32 [2, 24], replicated
- grad_d_skip: float32 [2, 24], replicated
- grad_out_gain: float32 [2, 1536], replicated
- grad_w_out: float32 [2, 1536, 768], P(None, 'shard')
Inputs may be any that keep to these rules, and one draw needn't show every extreme that they name: `lengths`: one sequence has exactly 512 tokens; the others at least a quarter of that.
All inputs are finite; a program needn't handle non-finite values.
Results may differ from a plain program's by a relative error of at most 0.011.
Values may be sent and summed in bfloat16 or wider, within the bound.
A program may use at most 208 MiB of HBM per device.

v0:
```python
import jax
import jax.numpy as jnp
from jax import lax
from jax.experimental import pallas as pl
from jax.experimental.pallas import tpu as pltpu
from jax.sharding import PartitionSpec as P

D = 768
DI = 1536
NH = 24
HEAD = 64
NSTATE = 128
KW = 4
CONV_CH = 1792
NIN = 3352
LAYERS = 2
MICRO = 2
CH = 128
PAIRS = NH // 2
LANE = 128
DUP = 32
LOG2E = 1.4426950408889634

epsilon = 1e-05
f32 = jnp.float32
bf16 = jnp.bfloat16
highest = lax.Precision.HIGHEST


def mm(a, b):
    return jnp.dot(a, b, preferred_element_type=f32)


def mm_t(a, b):
    return lax.dot_general(a, b, (((1,), (1,)), ((), ())), preferred_element_type=f32)


def t_mm(a, b):
    return lax.dot_general(a, b, (((0,), (0,)), ((), ())), preferred_element_type=f32)


def sigmoid(v):
    return 0.5 * jnp.tanh(0.5 * v) + 0.5


def softplus(v):
    return jnp.maximum(v, 0.0) + jnp.log1p(jnp.exp(-jnp.abs(v)))


def lanes(j, base=0):
    return slice(base + LANE * j, base + LANE * (j + 1))


def split_pair(v):
    left = lax.broadcasted_iota(jnp.int32, v.shape, 1) < HEAD
    zero = jnp.zeros_like(v)
    return jnp.concatenate([jnp.where(left, v, zero), jnp.where(left, zero, v)], axis=0)


def high_low(v):
    high = v.astype(bf16)
    return high, (v - high.astype(f32)).astype(bf16)


def widen(v, spread):
    high, low = high_low(v)
    first = lax.broadcasted_iota(jnp.int32, v.shape, 1) < DUP
    return mm(jnp.where(first, high, low), spread)


def step_parts(proj_ref, raw_ref, head_ref):
    raw = proj_ref[:, DI + CONV_CH :]
    raw_ref[:, 0:NH] = raw
    raw_ref[:, DUP : DUP + NH] = raw
    shifted = raw_ref[...] + head_ref[0:1]
    step = softplus(shifted)
    rows = lax.broadcasted_iota(jnp.int32, (CH, CH), 0)
    cols = lax.broadcasted_iota(jnp.int32, (CH, CH), 1)
    lower = (cols <= rows).astype(f32)
    cum = jnp.dot(lower, head_ref[1:2] * step, precision=highest, preferred_element_type=f32)
    grow = jnp.exp2(cum)
    remain = jnp.exp2(cum[CH - 1 : CH] - cum)
    return shifted, step, cum, cum.T, grow, remain, rows, cols


def conv_block(ext_ref, conv_ref, j):
    total = conv_ref[4:5, lanes(j)]
    for k in range(KW):
        total = total + conv_ref[k : k + 1, lanes(j)] * ext_ref[5 + k : 5 + k + CH, lanes(j)]
    return total


def forward_kernel(
    proj_ref, conv_ref, head_ref, wide_ref, spread_ref,
    mixed_ref, scan_ref, saved_ref,
    ext_ref, raw_ref, state_ref, gated_ref, keep_ref,
):
    @pl.when(pl.program_id(1) == 0)
    def _():
        state_ref[...] = jnp.zeros_like(state_ref)
        ext_ref[0:8] = jnp.zeros_like(ext_ref[0:8])

    @pl.when((pl.program_id(0) == 0) & (pl.program_id(1) == 0))
    def _():
        raw_ref[...] = jnp.zeros_like(raw_ref)

    ext_ref[8 : 8 + CH] = proj_ref[:, DI : DI + CONV_CH]
    shifted, step, cum, cum_t, grow, remain, rows, cols = step_parts(proj_ref, raw_ref, head_ref)
    spread = spread_ref[...]
    step_w = widen(step, spread)
    grow_w = widen(grow, spread)
    remain_w = widen(remain * step, spread)

    def activated(j):
        value = conv_block(ext_ref, conv_ref, j)
        return value * sigmoid(value)

    b_low = activated(PAIRS).astype(bf16)
    c_low = activated(PAIRS + 1).astype(bf16)
    affinity = jnp.where(cols <= rows, mm_t(c_low, b_low), 0.0)
    state_low = state_ref[...].astype(bf16)
    saved_ref[...] = state_low
    carried = grow_w * mm(c_low, state_low)
    square = jnp.zeros((CH, LANE), f32)
    for j in range(PAIRS):
        xs = activated(j)
        mixing = []
        for h in (2 * j, 2 * j + 1):
            differ = jnp.minimum(cum[:, h : h + 1] - cum_t[h : h + 1], 0.0)
            mixing.append((jnp.exp2(differ) * affinity).astype(bf16))
        keep_ref[:, lanes(j)] = (xs * remain_w[:, lanes(j)]).astype(bf16)
        x_split = split_pair((xs * step_w[:, lanes(j)]).astype(bf16))
        scanned = mm(jnp.concatenate(mixing, axis=1), x_split) + carried[:, lanes(j)]
        scan_ref[:, lanes(j)] = scanned
        gate = proj_ref[:, lanes(j)]
        gated = (scanned + wide_ref[0:1, lanes(j)] * xs) * (gate * sigmoid(gate))
        gated_ref[:, lanes(j)] = gated
        square = square + gated * gated
    state_ref[...] = grow_w[CH - 1 : CH] * state_ref[...] + t_mm(b_low, keep_ref[...])
    scale = lax.rsqrt(jnp.sum(square, axis=1, keepdims=True) * (1.0 / DI) + epsilon)
    mixed_ref[...] = (gated_ref[...] * scale * wide_ref[1:2]).astype(bf16)
    ext_ref[0:8] = ext_ref[CH : CH + 8]


def backward_kernel(
    proj_ref, tail_ref, scan_ref, saved_ref, grad_ref, conv_ref, head_ref, wide_ref, spread_ref, gather_ref,
    out_ref, sum_ref,
    ext_ref, raw_ref, state_ref, act_ref, slope_ref, gate_ref, dconv_ref, keep_ref, grown_ref, high_ref, low_ref, step_ref, row_ref,
):
    chunk = pl.num_programs(1) - 1 - pl.program_id(1)

    @pl.when(pl.program_id(1) == 0)
    def _():
        state_ref[...] = jnp.zeros_like(state_ref)
        dconv_ref[CH : CH + 8] = jnp.zeros_like(dconv_ref[CH : CH + 8])

    @pl.when((pl.program_id(0) == 0) & (pl.program_id(1) == 0))
    def _():
        raw_ref[...] = jnp.zeros_like(raw_ref)
        row_ref[...] = jnp.zeros_like(row_ref)
        sum_ref[...] = jnp.zeros_like(sum_ref)

    ext_ref[0:8] = jnp.where(chunk > 0, tail_ref[:, DI : DI + CONV_CH], 0.0)
    ext_ref[8 : 8 + CH] = proj_ref[:, DI : DI + CONV_CH]
    shifted, step, cum, cum_t, grow, remain, rows, cols = step_parts(proj_ref, raw_ref, head_ref)
    spread = spread_ref[...]
    step_w = widen(step, spread)
    grow_w = widen(grow, spread)
    remain_w = widen(remain, spread)

    square = jnp.zeros((CH, LANE), f32)
    along = jnp.zeros((CH, LANE), f32)
    for j in range(PAIRS + 2):
        value = conv_block(ext_ref, conv_ref, j)
        share = sigmoid(value)
        xs = value * share
        act_ref[:, lanes(j)] = xs
        slope_ref[:, lanes(j)] = share + xs * (1.0 - share)
        if j < PAIRS:
            gate = proj_ref[:, lanes(j)]
            open_share = sigmoid(gate)
            gate_ref[:, lanes(j)] = open_share
            gated = (scan_ref[:, lanes(j)] + wide_ref[0:1, lanes(j)] * xs) * (gate * open_share)
            square = square + gated * gated
            along = along + gated * (grad_ref[:, lanes(j)].astype(f32) * wide_ref[1:2, lanes(j)])
    scale = lax.rsqrt(jnp.sum(square, axis=1, keepdims=True) * (1.0 / DI) + epsilon)
    pull = scale * scale * scale * (jnp.sum(along, axis=1, keepdims=True) * (1.0 / DI))

    b_low = act_ref[:, lanes(PAIRS)].astype(bf16)
    c_low = act_ref[:, lanes(PAIRS + 1)].astype(bf16)
    affinity_t = jnp.where(rows <= cols, mm_t(b_low, c_low), 0.0)
    state = state_ref[...]
    state_low = state.astype(bf16)
    row_ref[1:2] = jnp.sum(saved_ref[...].astype(f32) * state, axis=0, keepdims=True)
    back = remain_w * mm(b_low, state_low)
    affinity_grad = jnp.zeros((CH, CH), f32)
    for j in range(PAIRS):
        xs = act_ref[:, lanes(j)]
        skip = wide_ref[0:1, lanes(j)]
        grad = grad_ref[:, lanes(j)].astype(f32)
        gate = proj_ref[:, lanes(j)]
        open_share = gate_ref[:, lanes(j)]
        opened = gate * open_share
        scanned = scan_ref[:, lanes(j)]
        outer = scanned + skip * xs
        gated = outer * opened
        gated_grad = scale * (grad * wide_ref[1:2, lanes(j)]) - pull * gated
        sum_ref[6:7, lanes(j)] += jnp.sum(grad * (gated * scale), axis=0, keepdims=True)
        dy = gated_grad * opened
        out_ref[:, lanes(j)] = (gated_grad * outer * (open_share + opened * (1.0 - open_share))).astype(bf16)
        sum_ref[5:6, lanes(j)] += jnp.sum(dy * xs, axis=0, keepdims=True)
        dy_low = dy.astype(bf16)
        grown_ref[:, lanes(j)] = (grow_w[:, lanes(j)] * dy).astype(bf16)
        scaled = xs * step_w[:, lanes(j)]
        x_low = scaled.astype(bf16)
        keep_ref[:, lanes(j)] = (scaled * remain_w[:, lanes(j)]).astype(bf16)
        dy_split = split_pair(dy_low)
        kernels = []
        for h in (2 * j, 2 * j + 1):
            differ = jnp.minimum(cum_t[h : h + 1] - cum[:, h : h + 1], 0.0)
            kernels.append(jnp.exp2(differ))
        mixing_t = jnp.concatenate([(k * affinity_t).astype(bf16) for k in kernels], axis=1)
        arrived = back[:, lanes(j)]
        x_grad = mm(mixing_t, dy_split) + arrived
        mixing_grad = mm_t(x_low, dy_split)
        affinity_grad = affinity_grad + mixing_grad[:, :CH] * kernels[0] + mixing_grad[:, CH:] * kernels[1]
        x_back = x_low.astype(f32)
        row_ref[0:1, lanes(j)] = jnp.sum(x_back * arrived, axis=0, keepdims=True)
        high, low = high_low(dy_low.astype(f32) * scanned - x_back * x_grad)
        high_ref[:, lanes(j)] = high
        low_ref[:, lanes(j)] = low
        step_ref[:, lanes(j)] = (x_grad * xs).astype(bf16)
        dconv_ref[0:CH, lanes(j)] = (step_w[:, lanes(j)] * x_grad + skip * dy) * slope_ref[:, lanes(j)]
    affinity_low = jnp.where(rows <= cols, affinity_grad, 0.0).astype(bf16)
    grown = grown_ref[...]
    b_grad = mm(affinity_low, c_low) + mm_t(keep_ref[...], state_low)
    c_grad = t_mm(affinity_low, b_low) + mm_t(grown, saved_ref[...])
    dconv_ref[0:CH, lanes(PAIRS)] = b_grad * slope_ref[:, lanes(PAIRS)]
    dconv_ref[0:CH, lanes(PAIRS + 1)] = c_grad * slope_ref[:, lanes(PAIRS + 1)]

    gather = gather_ref[...]
    row_high, row_low = high_low(row_ref[...])
    row_sums = mm(row_high, gather) + mm(row_low, gather)
    last_grad = row_sums[0:1] + grow[CH - 1 : CH] * row_sums[1:2]
    cum_grad = mm(high_ref[...], gather) + mm(low_ref[...], gather)
    upper = (cols >= rows).astype(f32)
    decay_grad = jnp.dot(upper, cum_grad, precision=highest, preferred_element_type=f32) + last_grad
    step_grad = mm(step_ref[...], gather) + head_ref[2:3] * decay_grad
    raw_grad = step_grad * sigmoid(shifted)
    out_ref[:, DI + CONV_CH :] = raw_grad[:, :NH].astype(bf16)
    sum_ref[7:8, 0:LANE] += jnp.sum(raw_grad, axis=0, keepdims=True)
    sum_ref[7:8, LANE : 2 * LANE] += jnp.sum(decay_grad * step, axis=0, keepdims=True)
    state_ref[...] = grow_w[CH - 1 : CH] * state + t_mm(c_low, grown)

    for j in range(PAIRS + 2):
        total = conv_ref[3:4, lanes(j)] * dconv_ref[0:CH, lanes(j)]
        for k in range(KW - 1):
            total = total + conv_ref[k : k + 1, lanes(j)] * dconv_ref[3 - k : 3 - k + CH, lanes(j)]
        out_ref[:, lanes(j, DI)] = total.astype(bf16)
        here = dconv_ref[0:CH, lanes(j)]
        for k in range(KW):
            sum_ref[k : k + 1, lanes(j)] += jnp.sum(here * ext_ref[5 + k : 5 + k + CH, lanes(j)], axis=0, keepdims=True)
        sum_ref[4:5, lanes(j)] += jnp.sum(here, axis=0, keepdims=True)
    dconv_ref[CH : CH + 8] = dconv_ref[0:8]


def fixed(shape):
    return pl.BlockSpec(shape, lambda r, c: (0,) * len(shape))


def mixer_forward(projected, tables, chunks):
    tokens = projected.shape[0]
    conv_t, head_t, wide_t, spread, _ = tables
    block = lambda r, c: (r * chunks + c, 0)
    return pl.pallas_call(
        forward_kernel,
        grid=(tokens // (chunks * CH), chunks),
        in_specs=[
            pl.BlockSpec((CH, NIN), block),
            fixed((8, CONV_CH)),
            fixed((8, LANE)),
            fixed((8, DI)),
            fixed((LANE, DI)),
        ],
        out_specs=[
            pl.BlockSpec((CH, DI), block),
            pl.BlockSpec((CH, DI), block),
            pl.BlockSpec((NSTATE, DI), block),
        ],
        out_shape=[
            jax.ShapeDtypeStruct((tokens, DI), bf16),
            jax.ShapeDtypeStruct((tokens, DI), f32),
            jax.ShapeDtypeStruct((tokens // CH * NSTATE, DI), bf16),
        ],
        scratch_shapes=[
            pltpu.VMEM((CH + 8, CONV_CH), f32),
            pltpu.VMEM((CH, LANE), f32),
            pltpu.VMEM((NSTATE, DI), f32),
            pltpu.VMEM((CH, DI), f32),
            pltpu.VMEM((CH, DI), bf16),
        ],
        compiler_params=pltpu.CompilerParams(
            dimension_semantics=("arbitrary", "arbitrary"), vmem_limit_bytes=48 * 2**20
        ),
        name="mixer_forward",
    )(projected, conv_t, head_t, wide_t, spread)


def mixer_backward(projected, scanned, saved, mixed_grad, tables, chunks):
    tokens = projected.shape[0]
    conv_t, head_t, wide_t, spread, gather = tables
    block = lambda r, c: (r * chunks + chunks - 1 - c, 0)
    ahead = lambda r, c: (jnp.maximum((r * chunks + chunks - 1 - c) * (CH // 8) - 1, 0), 0)
    return pl.pallas_call(
        backward_kernel,
        grid=(tokens // (chunks * CH), chunks),
        in_specs=[
            pl.BlockSpec((CH, NIN), block),
            pl.BlockSpec((8, NIN), ahead),
            pl.BlockSpec((CH, DI), block),
            pl.BlockSpec((NSTATE, DI), block),
            pl.BlockSpec((CH, DI), block),
            fixed((8, CONV_CH)),
            fixed((8, LANE)),
            fixed((8, DI)),
            fixed((LANE, DI)),
            fixed((DI, LANE)),
        ],
        out_specs=[
            pl.BlockSpec((CH, NIN), block),
            fixed((8, CONV_CH)),
        ],
        out_shape=[
            jax.ShapeDtypeStruct((tokens, NIN), bf16),
            jax.ShapeDtypeStruct((8, CONV_CH), f32),
        ],
        scratch_shapes=[
            pltpu.VMEM((CH + 8, CONV_CH), f32),
            pltpu.VMEM((CH, LANE), f32),
            pltpu.VMEM((NSTATE, DI), f32),
            pltpu.VMEM((CH, CONV_CH), f32),
            pltpu.VMEM((CH, CONV_CH), f32),
            pltpu.VMEM((CH, DI), f32),
            pltpu.VMEM((CH + 8, CONV_CH), f32),
            pltpu.VMEM((CH, DI), bf16),
            pltpu.VMEM((CH, DI), bf16),
            pltpu.VMEM((CH, DI), bf16),
            pltpu.VMEM((CH, DI), bf16),
            pltpu.VMEM((CH, DI), bf16),
            pltpu.VMEM((8, DI), f32),
        ],
        compiler_params=pltpu.CompilerParams(
            dimension_semantics=("arbitrary", "arbitrary"), vmem_limit_bytes=48 * 2**20
        ),
        name="mixer_backward",
    )(projected, projected, scanned, saved, mixed_grad, conv_t, head_t, wide_t, spread, gather)


def twice(v):
    return jnp.pad(jnp.concatenate([jnp.pad(v, (0, DUP - NH)), v]), (0, LANE - DUP - NH))


def mixer_tables(conv_w, conv_b, dt_bias, a_log, d_skip, out_gain):
    head = jnp.arange(DI) // HEAD
    column = jnp.arange(LANE)[:, None]
    spread = ((column % DUP == head[None]) & (column < 2 * DUP)).astype(bf16)
    rate = -jnp.exp(a_log)
    conv_t = jnp.concatenate([conv_w, conv_b[None], jnp.zeros((3, CONV_CH), f32)])
    head_t = jnp.concatenate(
        [jnp.stack([twice(dt_bias), twice(rate * LOG2E), twice(rate)]), jnp.zeros((5, LANE), f32)]
    )
    wide_t = jnp.concatenate([jnp.stack([jnp.repeat(d_skip, HEAD), out_gain]), jnp.zeros((6, DI), f32)])
    return conv_t, head_t, wide_t, spread, spread.T


def norm_parts(stream):
    return lax.rsqrt(jnp.mean(stream * stream, axis=-1, keepdims=True) + epsilon)


def shards(
    tokens, cotangent, lengths, dealing, in_gain, w_in, conv_w, conv_b, dt_bias, a_log, d_skip, out_gain, w_out,
):
    shard_count = lax.axis_size("shard")
    row_total = lax.axis_size("replica") * shard_count
    row_index = lax.axis_index("replica") * shard_count + lax.axis_index("shard")
    slot_count = tokens.shape[2]
    chunks = slot_count // CH
    token_count = MICRO * slot_count
    full_in = [lax.all_gather(w_in[l], "shard", axis=0, tiled=True) for l in range(LAYERS)]
    full_out = [lax.all_gather(w_out[l], "shard", axis=0, tiled=True) for l in range(LAYERS)]
    global_rows = jnp.arange(MICRO) * row_total + row_index
    sequence = jnp.sum(jnp.where(jnp.arange(dealing.shape[0])[None] == global_rows[:, None], dealing[None], 0), axis=1)
    seq_length = jnp.sum(jnp.where(jnp.arange(lengths.shape[0])[None] == sequence[:, None], lengths[None], 0), axis=1)
    valid = (jnp.arange(slot_count)[None] < seq_length[:, None]).astype(f32).reshape(token_count, 1)

    stream = tokens.reshape(token_count, D).astype(f32)
    saved = []
    for l in range(LAYERS):
        normed = (stream * norm_parts(stream) * in_gain[l]).astype(bf16)
        projected = mm(normed, full_in[l])
        tables = mixer_tables(conv_w[l], conv_b[l], dt_bias[l], a_log[l], d_skip[l], out_gain[l])
        mixed, scanned, states = mixer_forward(projected, tables, chunks)
        saved.append((stream, normed, projected, tables, mixed, scanned, states))
        stream = stream + mm(mixed, full_out[l])
    result = (stream * valid).astype(bf16)

    upstream = cotangent.reshape(token_count, D).astype(f32) * valid
    in_grads = [None] * LAYERS
    out_grads = [None] * LAYERS
    gain_grads = [None] * LAYERS
    sums = [None] * LAYERS
    for l in reversed(range(LAYERS)):
        entered, normed, projected, tables, mixed, scanned, states = saved[l]
        branch_grad = upstream.astype(bf16)
        out_grads[l] = lax.psum_scatter(t_mm(mixed, branch_grad).astype(bf16), "shard", scatter_dimension=0, tiled=True)
        mixed_grad = mm_t(branch_grad, full_out[l]).astype(bf16)
        project_grad, sums[l] = mixer_backward(projected, scanned, states, mixed_grad, tables, chunks)
        in_grads[l] = lax.psum_scatter(t_mm(normed, project_grad).astype(bf16), "shard", scatter_dimension=0, tiled=True)
        normed_grad = mm_t(project_grad, full_in[l])
        scale = norm_parts(entered)
        gain_grads[l] = jnp.sum(normed_grad * entered * scale, axis=0)
        inner = normed_grad * in_gain[l]
        pull = scale * scale * scale * jnp.mean(inner * entered, axis=-1, keepdims=True)
        upstream = upstream + scale * inner - pull * entered
    in_total = lax.psum(jnp.stack(in_grads).astype(f32), "replica")
    out_total = lax.psum(jnp.stack(out_grads).astype(f32), "replica")
    small, gain_total = lax.psum((jnp.stack(sums), jnp.stack(gain_grads)), ("replica", "shard"))
    rate = -jnp.exp(a_log)
    shape = (MICRO, 1, slot_count, D)
    return (
        result.reshape(shape),
        upstream.reshape(shape),
        gain_total,
        in_total,
        small[:, 0:4],
        small[:, 4],
        small[:, 7, 0:NH],
        small[:, 7, LANE : LANE + NH] * rate,
        small[:, 5, :DI].reshape(LAYERS, NH, HEAD).sum(-1),
        small[:, 6, :DI],
        out_total,
    )


def solution(mesh):
    rows = P(None, ("replica", "shard"), None, None)
    split = P(None, "shard", None)
    in_specs = (rows, rows, P(), P(), P(), split, P(), P(), P(), P(), P(), P(), split)
    out_specs = (rows, rows, P(), split, P(), P(), P(), P(), P(), P(), split)
    return jax.shard_map(shards, mesh=mesh, in_specs=in_specs, out_specs=out_specs, check_vma=False)
```

profile of v0, /device:TPU:0, one launch (start us, length us, event | category | flops | bytes accessed | tf_op | source)
XLA Modules:
  0.0 760.9 jit_solution(5367499102661248815)
XLA Ops:
  7.3 2.0 fusion.39
  9.4 2.4 fusion.38
  15.1 2.9 fusion.9
  20.3 22.0 %all-gather.15.cloned.1.call-done = bf16[1,1536,768]{2,1,0:T(8,128)(2,1)} async-done(((bf16[1,192,768]{2,1,0:T(8,128)(2,1)}), bf16[1,1536,768]{2,1,0:T(8,128)(2,1)}) %all-gather.15.cloned.1.call-update) | async-done | bytes 2359312 | tf_op jit(solution)/shard_map/all_gather | solution.py:390
  42.3 6.5 convolution_convert_fusion.3.grad_ref
  48.7 37.4 %all-gather.9.cloned.1.call-done = bf16[1,768,3352]{2,1,0:T(8,128)(2,1)} async-done(((bf16[1,96,3352]{2,1,0:T(8,128)(2,1)}), bf16[1,768,3352]{2,1,0:T(8,128)(2,1)}) %all-gather.9.cloned.1.call-update) | async-done | bytes 5148688 | tf_op jit(solution)/shard_map/all_gather | solution.py:389
  86.1 11.9 %fusion.6.proj_ref.tail_ref = f32[1024,3352]{1,0:T(8,128)} fusion(bf16[1024,768]{1,0:T(8,128)(2,1)} %fusion.13, bf16[1,768,3352]{2,1,0:T(8,128)(2,1)} %all-gather.9.cloned.1.call-done), kind=kOutput, calls=%fused_computation.8 | convolution fusion | flops 5272240128 | bytes 20451328 | tf_op jit(solution)/shard_map/dot_general | solution.py:31
  98.0 23.0 %mixer_forward.2 = (bf16[1024,1536]{1,0:T(8,128)(2,1)S(1)}, f32[1024,1536]{1,0:T(8,128)}, bf16[1024,1536]{1,0:T(8,128)(2,1)}) custom-call(f32[1024,3352]{1,0:T(8,128)} %fusion.6.proj_ref.tail_ref, f32[8,1792]{1,0:T(8,128)S(1)} %get-tuple-element.88.conv_ref, f32[8,128]{1,0:T(8,128)S(1)} %get-tuple-element.86.head_ref, ...), custom_call_target="tpu_custom_call" | custom-call | tf_op jit(solution)/shard_map/mixer_forward/pallas_call | solution.py:275
  122.7 7.0 multiply_reduce_fusion.2
  129.7 31.1 %all-gather.13.cloned.1.call-done = bf16[1,768,3352]{2,1,0:T(8,128)(2,1)} async-done(((bf16[1,96,3352]{2,1,0:T(8,128)(2,1)}), bf16[1,768,3352]{2,1,0:T(8,128)(2,1)}) %all-gather.13.cloned.1.call-update) | async-done | bytes 5148688 | tf_op jit(solution)/shard_map/all_gather | solution.py:389
  160.8 12.2 %fusion.2.proj_ref.tail_ref = f32[1024,3352]{1,0:T(8,128)} fusion(bf16[1,768,3352]{2,1,0:T(8,128)(2,1)} %all-gather.13.cloned.1.call-done, f32[1024,768]{1,0:T(8,128)} %get-tuple-element.90, f32[768]{0:T(1024)S(1)} %get-tuple-element.57, f32[1024]{0:T(1024)S(1)} %add_rsqrt_fusion), kind=kOutput, calls=%fused_computation.4 | convolution fusion | flops 5274599424 | bytes 22031360 | tf_op jit(solution)/shard_map/dot_general | solution.py:31
  173.0 23.2 %mixer_forward.3 = (bf16[1024,1536]{1,0:T(8,128)(2,1)S(1)}, f32[1024,1536]{1,0:T(8,128)}, bf16[1024,1536]{1,0:T(8,128)(2,1)}) custom-call(f32[1024,3352]{1,0:T(8,128)} %fusion.2.proj_ref.tail_ref, f32[8,1792]{1,0:T(8,128)S(1)} %get-tuple-element.87.conv_ref, f32[8,128]{1,0:T(8,128)S(1)} %get-tuple-element.85.head_ref, ...), custom_call_target="tpu_custom_call" | custom-call | tf_op jit(solution)/shard_map/mixer_forward/pallas_call | solution.py:275
  199.8 49.3 %mixer_backward.2 = (bf16[1024,3352]{1,0:T(8,128)(2,1)}, f32[8,1792]{1,0:T(8,128)S(1)}) custom-call(f32[1024,3352]{1,0:T(8,128)} %fusion.2.proj_ref.tail_ref, f32[1024,3352]{1,0:T(8,128)} %fusion.2.proj_ref.tail_ref, f32[1024,1536]{1,0:T(8,128)} %get-tuple-element.23.scan_ref, bf16[1024,1536]{1,0:T(8,128)(2,1)S(1)} %copy-done.1, ...), custom_call_target="tpu_custom_call" | custom-call | tf_op jit(solution)/shard_map/mixer_backward/pallas_call | solution.py:314
  249.2 8.6 %multiply_reduce_fusion = (f32[768]{0:T(1024)S(1)}, f32[1024]{0:T(1024)S(1)}, f32[1024,768]{1,0:T(8,128)S(1)}) fusion(f32[1024,768]{1,0:T(8,128)S(1)} %copy-done.9, f32[1024]{0:T(1024)S(1)} %add_rsqrt_fusion, f32[768]{0:T(1024)S(1)} %get-tuple-element.57, bf16[1024,3352]{1,0:T(8,128)(2,1)} %get-tuple-element.25, bf16[1,768,3352]{2,1,0:T(8,128)(2,1)S(1)} %bitcast.141), kind=kOutput, calls=%fused_computation.31 | convolution fusion | flops 5276956672 | bytes 18319360 | tf_op jit(solution)/shard_map/dot_general | solution.py:35
  260.6 4.0 convolution_convert_fusion.5
  264.8 6.4 convolution_convert_fusion.4
  271.4 11.9 %convolution_convert_fusion = bf16[768,3352]{1,0:T(8,128)(2,1)} fusion(bf16[1024,3352]{1,0:T(8,128)(2,1)} %get-tuple-element.25, f32[1024,768]{1,0:T(8,128)} %get-tuple-element.90, f32[768]{0:T(1024)S(1)} %get-tuple-element.57, f32[1024]{0:T(1024)S(1)} %add_rsqrt_fusion), kind=kOutput, calls=%fused_computation | convolution fusion | flops 5277173760 | bytes 15166464 | tf_op jit(solution)/shard_map/dot_general | solution.py:39
  283.4 7.1 convolution_convert_fusion.2.grad_ref
  290.4 48.8 %mixer_backward.3 = (bf16[1024,3352]{1,0:T(8,128)(2,1)}, f32[8,1792]{1,0:T(8,128)S(1)}) custom-call(f32[1024,3352]{1,0:T(8,128)} %fusion.6.proj_ref.tail_ref, f32[1024,3352]{1,0:T(8,128)} %fusion.6.proj_ref.tail_ref, f32[1024,1536]{1,0:T(8,128)} %get-tuple-element.26.scan_ref, bf16[1024,1536]{1,0:T(8,128)(2,1)S(1)} %copy-done, ...), custom_call_target="tpu_custom_call" | custom-call | tf_op jit(solution)/shard_map/mixer_backward/pallas_call | solution.py:314
  339.2 10.7 %convolution_convert_fusion.1 = bf16[768,3352]{1,0:T(8,128)(2,1)} fusion(bf16[1024,768]{1,0:T(8,128)(2,1)S(1)} %copy-done.11, bf16[1024,3352]{1,0:T(8,128)(2,1)} %get-tuple-element.28), kind=kOutput, calls=%fused_computation.1 | convolution fusion | flops 5274814464 | bytes 13586432 | tf_op jit(solution)/shard_map/dot_general | solution.py:39
  351.0 2.9 reduce-scatter.11.cloned.1.call-done
  353.9 2.1 maximum_convert_fusion.1
  356.1 58.2 %reduce-scatter.7.cloned.1.call-done = bf16[96,3352]{1,0:T(8,128)(2,1)} async-done(((bf16[768,3352]{1,0:T(8,128)(2,1)}), bf16[96,3352]{1,0:T(8,128)(2,1)}) %reduce-scatter.7.cloned.1.call-update) | async-done | bytes 643600 | tf_op jit(solution)/shard_map/reduce_scatter | solution.py:418
  414.3 60.8 %reduce-scatter.5.cloned.1.call-done = bf16[96,3352]{1,0:T(8,128)(2,1)} async-done(((bf16[768,3352]{1,0:T(8,128)(2,1)}), bf16[96,3352]{1,0:T(8,128)(2,1)}) %reduce-scatter.5.cloned.1.call-update) | async-done | bytes 643600 | tf_op jit(solution)/shard_map/reduce_scatter | solution.py:418
  475.0 3.0 maximum_convert_fusion
  478.0 11.1 %fusion.17 = (f32[768]{0:T(1024)S(1)}, f32[1024]{0:T(1024)S(1)}, f32[1024,768]{1,0:T(8,128)}) fusion(bf16[2,1,512,768]{3,2,1,0:T(8,128)(2,1)S(1)} %copy-done.6, f32[1024]{0:T(1024)S(1)} %bitcast.130, f32[768]{0:T(1024)S(1)} %get-tuple-element.58, bf16[1024,3352]{1,0:T(8,128)(2,1)} %get-tuple-element.28, bf16[1,768,3352]{2,1,0:T(8,128)(2,1)} %all-gather.9.cloned.1.call-done), kind=kOutput, calls=%fused_computation.30 | convolution fusion | flops 5277743104 | bytes 16746496 | tf_op jit(solution)/shard_map/dot_general | solution.py:35
  489.2 39.4 %psum.28 = f32[2,768]{1,0:T(2,128)} all-reduce(f32[2,768]{1,0:T(2,128)S(1)} %pad_maximum_fusion.1), channel_id=1, replica_groups=mesh['replica'=4,'shard'=8] {'replica','shard'}, use_global_device_ids=true, to_apply=%region_8.9 | all-reduce | flops 1536 | bytes 12288 | tf_op jit(solution)/shard_map/psum | solution.py:427
  528.6 5.4 fusion.15
  535.2 3.7 multiply_convert_fusion
  538.8 62.5 %all-reduce.16.cloned.1.call-done = f32[2,8,1792]{2,1,0:T(8,128)} async-done(((f32[2,8,1792]{2,1,0:T(8,128)}), f32[2,8,1792]{2,1,0:T(8,128)}) %all-reduce.16.cloned.1.call-update) | async-done | bytes 114704 | tf_op jit(solution)/shard_map/psum | solution.py:427
  608.6 140.6 %all-reduce.18.cloned.1.call-done = (f32[2,96,3352]{2,1,0:T(8,128)}, f32[2,192,768]{2,1,0:T(8,128)}) async-done(((f32[2,96,3352]{2,1,0:T(8,128)}, f32[2,192,768]{2,1,0:T(8,128)}), (f32[2,96,3352]{2,1,0:T(8,128)}, f32[2,192,768]{2,1,0:T(8,128)})) %all-reduce.18.cloned.1.call-update) | async-done | bytes 3754000 | tf_op jit(solution)/shard_map/psum | solution.py:425
  749.3 3.5 copy.53
  (135 shorter events, 24.4 us)
Async XLA Ops:
  7.2 6.3 copy-start.18
  7.2 6.3 copy-start.21
  7.2 6.5 copy-start.22
  7.2 6.7 copy-start.6
  7.2 35.0 %all-gather.15.cloned.1.call-start = ((), (), s32[]{:S(2)}) async-start(), calls=%async_computation.12 | async-start | bytes 2654208 | tf_op jit(solution)/shard_map/all_gather | solution.py:390
  9.3 5.4 copy-start.19
  9.3 5.5 copy-start.16
  9.3 5.7 copy-start.17
  9.3 76.8 %all-gather.9.cloned.1.call-start = ((), (), s32[]{:S(2)}) async-start(), calls=%async_computation.9 | async-start | bytes 5971968 | tf_op jit(solution)/shard_map/all_gather | solution.py:389
  11.8 110.8 %all-gather.11.cloned.1.call-start = ((), (), s32[]{:S(2)}) async-start(), calls=%async_computation.10 | async-start | bytes 2654208 | tf_op jit(solution)/shard_map/all_gather | solution.py:390
  12.6 148.2 %all-gather.13.cloned.1.call-start = ((), (), s32[]{:S(2)}) async-start(), calls=%async_computation.11 | async-start | bytes 5971968 | tf_op jit(solution)/shard_map/all_gather | solution.py:389
  13.1 337.9 %reduce-scatter.9.cloned.1.call-start = ((), (), s32[]{:S(2)}) async-start(), calls=%async_computation.7 | async-start | bytes 2654208 | tf_op jit(solution)/shard_map/reduce_scatter | solution.py:415
  15.1 4.5 copy-start.15
  15.1 4.5 copy-start.14
  15.1 4.5 copy-start.13
  173.0 76.1 %slice-start = ((s8[5308416]{0:T(1024)(128)(4,1)}), s8[4194304]{0:T(1024)(128)(4,1)S(1)}, s32[]{:S(2)}) async-start(s8[5308416]{0:T(1024)(128)(4,1)} %bitcast.140), calls=%async_computation.14 | async-start | bytes 8388608
  197.9 1.9 copy-start.1
  199.8 49.3 %copy-start.9 = (f32[1024,768]{1,0:T(8,128)S(1)}, f32[1024,768]{1,0:T(8,128)}, u32[]{:S(2)}) copy-start(f32[1024,768]{1,0:T(8,128)} %get-tuple-element.90) | copy-start | bytes 9437188
  199.8 49.3 %slice-start.1 = ((s8[5308416]{0:T(1024)(128)(4,1)}), s8[1114112]{0:T(1024)(128)(4,1)S(1)}, s32[]{:S(2)}) async-start(s8[5308416]{0:T(1024)(128)(4,1)} %bitcast.140), calls=%async_computation.15 | async-start | bytes 2228224
  249.2 8.6 %copy-start.8 = (bf16[2,1,512,768]{3,2,1,0:T(8,128)(2,1)S(1)}, bf16[2,1,512,768]{3,2,1,0:T(8,128)(2,1)}, u32[]{:S(2)}) copy-start(bf16[2,1,512,768]{3,2,1,0:T(8,128)(2,1)} %param.14) | copy-start | bytes 4718596
  257.8 2.8 copy-start.5
  264.6 89.3 %reduce-scatter.11.cloned.1.call-start = ((), (), s32[]{:S(2)}) async-start(), calls=%async_computation.8 | async-start | bytes 2654208 | tf_op jit(solution)/shard_map/reduce_scatter | solution.py:415
  271.3 142.9 %reduce-scatter.7.cloned.1.call-start = ((), (), s32[]{:S(2)}) async-start(), calls=%async_computation.5 | async-start | bytes 5971968 | tf_op jit(solution)/shard_map/reduce_scatter | solution.py:418
  283.3 191.7 %reduce-scatter.5.cloned.1.call-start = ((), (), s32[]{:S(2)}) async-start(), calls=%async_computation.4 | async-start | bytes 5971968 | tf_op jit(solution)/shard_map/reduce_scatter | solution.py:418
  283.4 7.1 copy-start
  290.4 48.8 %copy-start.11 = (bf16[1024,768]{1,0:T(8,128)(2,1)S(1)}, bf16[1024,768]{1,0:T(8,128)(2,1)}, u32[]{:S(2)}) copy-start(bf16[1024,768]{1,0:T(8,128)(2,1)} %fusion.13) | copy-start | bytes 4718596
  350.0 251.4 %all-reduce.16.cloned.1.call-start = ((), (), s32[]{:S(2)}) async-start(), calls=%async_computation.6 | async-start | bytes 229376 | tf_op jit(solution)/shard_map/psum | solution.py:427
  350.7 398.5 %all-reduce.18.cloned.1.call-start = ((), (), s32[]{:S(2)}) async-start(), calls=%async_computation.13 | async-start | bytes 7667712 | tf_op jit(solution)/shard_map/psum | solution.py:425
  528.6 5.4 copy-start.3
  528.6 5.4 copy-start.10
  528.6 6.5 copy-start.20
  749.3 3.5 copy-start.12
  (3 other events, 5.0 us)
Sparse Core Ops, SparseCore 0:
  10.5 31.7 all-gather.14
  44.7 41.3 all-gather.8
  88.0 29.0 all-gather.10
  119.4 41.3 all-gather.12
  264.7 42.4 reduce-scatter.8
  311.4 42.4 reduce-scatter.10
  357.3 56.8 reduce-scatter.6
  418.0 56.9 reduce-scatter.4
  480.6 120.7 all-reduce.15
  604.8 144.3 all-reduce.17
where the time goes:
time: 765 us; the launch traced here: 761 us
  waiting for transfers between devices  417 us (55%)
  Pallas kernels  144 us (19%)
  matrix products  101 us (13%)
  blocking collectives  39.4 us (5%)
  local copies, waits for them, and re-layouts  23.8 us (3%)
  other arithmetic  19.8 us (3%)
  between operations  14.8 us (2%)
    psum x1, waiting for transfers between devices, shards(): in_total = lax.psum(jnp.stack(in_grads).astype(f32), 'replica')  141 us
    reduce_scatter x2, waiting for transfers between devices, shards(): lax.psum_scatter(t_mm(normed, project_grad).astype(bf16), 'shard', scatte...  119 us
    pallas_call x2, Pallas kernels, mixer_backward(): pl.pallas_call(backward_kernel, grid=(tokens // (chunks * CH), chunks), i...  98.1 us
    all_gather x2, waiting for transfers between devices, shards(): lax.all_gather(w_in[l], 'shard', axis=0, tiled=True)  68.6 us
    psum x1, waiting for transfers between devices, shards(): lax.psum((jnp.stack(sums), jnp.stack(gain_grads)), ('replica', 'shard'))  62.5 us
    pallas_call x2, Pallas kernels, mixer_forward(): pl.pallas_call(forward_kernel, grid=(tokens // (chunks * CH), chunks), in...  46.1 us
    psum x1, blocking collectives, shards(): lax.psum((jnp.stack(sums), jnp.stack(gain_grads)), ('replica', 'shard'))  39.4 us
    dot_general x4, matrix products, mm(): return jnp.dot(a, b, preferred_element_type=f32)  34.8 us
  transfers between devices with their start and end apart: 10, of which 8 were waited for; matrix products, arithmetic and copies ran while one was open for 14% of the time, Pallas kernels for 9%

commit v1 on v0

--- a/solution.py
+++ b/solution.py
@@ -25,6 +25,7 @@
 f32 = jnp.float32
 bf16 = jnp.bfloat16
 highest = lax.Precision.HIGHEST
+MESH = pl.DeviceIdType.MESH
 
 
 def mm(a, b):
@@ -356,6 +357,233 @@
     )(projected, projected, scanned, saved, mixed_grad, conv_t, head_t, wide_t, spread, gather)
 
 
+def ring_place(n):
+    wide = n // 4
+    me = lax.axis_index("shard")
+    chip, core = me // 2, me % 2
+    row, col = chip // wide, chip % wide
+    place = row * col_last(wide, col) + (1 - row) * col
+    def shard_of(p, c):
+        p = p % (2 * wide)
+        r = p // wide
+        x = r * (2 * wide - 1 - p) + (1 - r) * p
+        return (r * wide + x) * 2 + c
+    return place, core, shard_of
+
+def col_last(wide, col):
+    return 2 * wide - 1 - col
+
+def halves(rows):
+    first = rows // 2 // 16 * 16
+    return (0, first), (first, rows - first)
+
+def gather_kernel(n, *refs):
+    count = (len(refs) - 4) // 2
+    parts, wholes = refs[:count], refs[count:2*count]
+    send_sem, recv_sem, pair_sem, own_sem = refs[2*count:]
+    half = n // 4
+    place, core, shard_of = ring_place(n)
+    right, left, pair = shard_of(place + 1, core), shard_of(place + n // 2 - 1, core), shard_of(place, 1 - core)
+    barrier = pltpu.get_barrier_semaphore()
+    for to in (right, left, pair):
+        pl.semaphore_signal(barrier, inc=1, device_id={"shard": to}, device_id_type=MESH)
+    pl.semaphore_wait(barrier, 3)
+    def span(a, owner, part):
+        rows = parts[a].shape[0]
+        start, size = part
+        return pl.ds(pl.multiple_of(owner * rows + start, 16), size)
+    sent = []
+    def send(a, src, owner, part, to, sems, k):
+        rows = span(a, owner, part)
+        c = pltpu.make_async_remote_copy(src_ref=src if src is not None else wholes[a].at[rows], dst_ref=wholes[a].at[rows],
+            send_sem=sems[0], recv_sem=sems[1], device_id={"shard": to}, device_id_type=MESH)
+        c.start(); sent.append(c)
+        return c
+    me = shard_of(place, core)
+    local = []
+    for a in range(count):
+        whole = (0, parts[a].shape[0])
+        c = pltpu.make_async_copy(parts[a], wholes[a].at[span(a, me, whole)], own_sem.at[a]); c.start(); local.append(c)
+    got = {}
+    pairs = []
+    k = 0
+    def piece_rows(a, s, d):
+        rows = parts[a].shape[0]
+        return (0, rows) if s < half else halves(rows)[d]
+    for a in range(count):
+        for d, to in ((0, right), (1, left)):
+            got[a, 1, d] = send(a, parts[a], me, piece_rows(a, 1, d), to, (send_sem.at[a, 0, d], recv_sem.at[a, 0, d]), 0) if half > 1 else None
+        pairs.append(send(a, parts[a], me, (0, parts[a].shape[0]), pair, (send_sem.at[a, half, 0], pair_sem.at[a, 0, 0]), 0))
+    for s in range(1, half + 1):
+        for a in range(count):
+            for d, to in ((0, right), (1, left)):
+                got[a, s, d].wait_recv()
+                owner = shard_of(place + (n // 2 - s if d == 0 else s), core)
+                rows = piece_rows(a, s, d)
+                if s < half:
+                    ahead = piece_rows(a, s + 1, d)
+                    got[a, s + 1, d] = send(a, None, owner, ahead, to, (send_sem.at[a, s, d], recv_sem.at[a, s, d]), 0)
+                pairs.append(send(a, None, owner, rows, pair, (send_sem.at[a, half + s, d], pair_sem.at[a, s, d]), 0))
+    for c in pairs: c.wait_recv()
+    for c in sent: c.wait_send()
+    for c in local: c.wait()
+
+def gather(parts, n, collective_id):
+    count=len(parts); half=n//4
+    return pl.pallas_call(
+        lambda *refs: gather_kernel(n, *refs),
+        out_shape=[jax.ShapeDtypeStruct((p.shape[0]*n, p.shape[1]), p.dtype) for p in parts],
+        in_specs=[pl.BlockSpec(memory_space=pl.ANY)]*count, out_specs=[pl.BlockSpec(memory_space=pl.ANY)]*count,
+        scratch_shapes=[pltpu.SemaphoreType.DMA((count, 2*half+1, 2)), pltpu.SemaphoreType.DMA((count, half, 2)),
+            pltpu.SemaphoreType.DMA((count, half+1, 2)), pltpu.SemaphoreType.DMA((count,))],
+        compiler_params=pltpu.CompilerParams(collective_id=collective_id, has_side_effects=True),
+        name="gather_first",
+    )(*parts)
+
+def column_groups(width, replicas, parts):
+    unit = 128 * replicas
+    units = -(-width // unit)
+    parts = min(parts, units)
+    groups, start = [], 0
+    for g in range(parts):
+        size = (units // parts + (g < units % parts)) * unit
+        groups.append((start, size, min(size, width - start)))
+        start += size
+    return groups, start
+
+def reduce_kernel(n, replicas, groups, grad_ref, small_ref, out_ref, total_ref,
+    pair_buf, out_buf, in_buf, sum_buf, cross_buf, share_buf, whole_buf, small_buf, small_cross,
+    pair_send, pair_recv, ring_send, ring_recv, cross_send, cross_recv, share_send, share_recv, small_sems, cross_sems):
+    chips = n // 2
+    half = chips // 2
+    rows = grad_ref.shape[0] // n
+    place, core, shard_of = ring_place(n)
+    right, left, pair = shard_of(place + 1, core), shard_of(place + chips - 1, core), shard_of(place, 1 - core)
+    me, mine = lax.axis_index("shard"), lax.axis_index("replica")
+    barrier = pltpu.get_barrier_semaphore()
+    for s in range(1, n):
+        pl.semaphore_signal(barrier, inc=1, device_id={"shard": (me + s) % n}, device_id_type=MESH)
+    for s in range(1, replicas):
+        pl.semaphore_signal(barrier, inc=1, device_id={"replica": (mine + s) % replicas}, device_id_type=MESH)
+    pl.semaphore_wait(barrier, n + replicas - 2)
+    started = []
+    def copy(src, dst, send, recv, to):
+        c = pltpu.make_async_remote_copy(src_ref=src, dst_ref=dst, send_sem=send, recv_sem=recv, device_id=to, device_id_type=MESH)
+        c.start(); started.append(c)
+        return c
+    def piece(owner, cols, part=None):
+        start, size = part if part is not None else (0, rows)
+        return pl.ds(pl.multiple_of(owner * rows + start, 16), size), cols
+    order = [half] + [v for s in range(half - 1, 0, -1) for v in (s, chips - s)] + [0]
+    paired = {}
+    for g, (start, size, wide) in enumerate(groups):
+        cols = slice(start, start + wide)
+        for q in order:
+            owner = shard_of(place + q, 1 - core)
+            paired[g, q] = copy(grad_ref.at[piece(owner, cols)], pair_buf.at[q, :, cols], pair_send.at[g, q], pair_recv.at[g, q], {"shard": pair})
+        if g == 0:
+            small = [copy(small_ref, small_buf.at[s], small_sems.at[0, s], small_sems.at[1, s], {"shard": (me + s) % n}) for s in range(1, n)]
+    def own(g, q, part):
+        start, size, wide = groups[g]
+        cols = slice(start, start + wide)
+        first, count = part
+        return grad_ref[piece(shard_of(place + q, core), cols, part)].astype(f32) + pair_buf[q, first:first + count, cols].astype(f32)
+    ring = {}
+    every = (0, rows)
+    for k in range(1, half + 1):
+        for g, (start, size, wide) in enumerate(groups):
+            cols = slice(start, start + wide)
+            for d, to in ((0, right), (1, left)):
+                q = half - k + 1 if d == 0 else chips - (half - k + 1)
+                if k == 1:
+                    if d == 0: paired[g, q].wait_recv()
+                    part = halves(rows)[d]
+                    first, count = part
+                    out_buf[k - 1, d, first:first + count, cols] = own(g, q, part).astype(bf16)
+                else:
+                    part = every
+                    first, count = part
+                    paired[g, q].wait_recv()
+                    ring[g, k - 1, d].wait_recv()
+                    if k == 2:
+                        for e in (0, 1):
+                            at, many = halves(rows)[e]
+                            value = own(g, q, (at, many))
+                            if e == d: value = value + in_buf[k - 2, d, at:at + many, cols].astype(f32)
+                            out_buf[k - 1, d, at:at + many, cols] = value.astype(bf16)
+                    else:
+                        out_buf[k - 1, d, :, cols] = (own(g, q, every) + in_buf[k - 2, d, :, cols].astype(f32)).astype(bf16)
+                ring[g, k, d] = copy(out_buf.at[k - 1, d, first:first + count, cols], in_buf.at[k - 1, d, first:first + count, cols],
+                    ring_send.at[g, k - 1, d], ring_recv.at[g, k - 1, d], {"shard": to})
+        if k == 1:
+            for c in small: c.wait_recv()
+            small_buf[0] = small_ref[...]
+            def add(i, acc):
+                return acc + small_buf[(me - i + n) % n]
+            small_cross[0] = lax.fori_loop(0, n, add, jnp.zeros(small_ref.shape, f32))
+            across = [copy(small_cross.at[0], small_cross.at[s], cross_sems.at[0, s], cross_sems.at[1, s], {"replica": (mine + s) % replicas}) for s in range(1, replicas)]
+    cross = {}
+    for g, (start, size, wide) in enumerate(groups):
+        cols = slice(start, start + wide)
+        paired[g, 0].wait_recv()
+        ring[g, half, 0].wait_recv(); ring[g, half, 1].wait_recv()
+        value = own(g, 0, every) + in_buf[half - 1, 0, :, cols].astype(f32) + in_buf[half - 1, 1, :, cols].astype(f32)
+        sum_buf[:, cols] = value.astype(bf16)
+        if wide < size:
+            sum_buf[:, start + wide:start + size] = jnp.zeros((rows, size - wide), bf16)
+        each = size // replicas
+        at = start // replicas
+        for s in range(1, replicas):
+            to = (mine + s) % replicas
+            cross[g, s] = copy(sum_buf.at[:, pl.ds(pl.multiple_of(start + to * each, 128), each)], cross_buf.at[s, :, at:at + each],
+                cross_send.at[g, s], cross_recv.at[g, s], {"replica": to})
+    shared = {}
+    for g, (start, size, wide) in enumerate(groups):
+        each = size // replicas
+        at = start // replicas
+        for s in range(1, replicas): cross[g, s].wait_recv()
+        cross_buf[0, :, at:at + each] = sum_buf[:, pl.ds(pl.multiple_of(start + mine * each, 128), each)]
+        value = cross_buf[0, :, at:at + each].astype(f32)
+        for s in range(1, replicas): value = value + cross_buf[s, :, at:at + each].astype(f32)
+        share_buf[:, at:at + each] = value.astype(bf16)
+        for s in range(1, replicas):
+            to = (mine + s) % replicas
+            shared[g, s] = copy(share_buf.at[:, at:at + each], whole_buf.at[:, pl.ds(pl.multiple_of(start + mine * each, 128), each)],
+                share_send.at[g, s], share_recv.at[g, s], {"replica": to})
+        whole_buf[:, pl.ds(pl.multiple_of(start + mine * each, 128), each)] = share_buf[:, at:at + each]
+    for c in across: c.wait_recv()
+    def add_cross(i, acc):
+        return acc + small_cross[(mine - i + replicas) % replicas]
+    total_ref[...] = lax.fori_loop(0, replicas, add_cross, jnp.zeros(small_ref.shape, f32))
+    for g, (start, size, wide) in enumerate(groups):
+        for s in range(1, replicas): shared[g, s].wait_recv()
+        cols = slice(start, start + wide)
+        out_ref[:, cols] = whole_buf[:, cols].astype(f32)
+    for c in started: c.wait_send()
+
+def reduce_last(grad, small, n, replicas, collective_id, parts=3):
+    total, width = grad.shape
+    rows = total // n
+    chips, half = n // 2, n // 4
+    groups, padded = column_groups(width, replicas, parts)
+    count = len(groups)
+    dma = pltpu.SemaphoreType.DMA
+    return pl.pallas_call(
+        lambda *refs: reduce_kernel(n, replicas, groups, *refs),
+        out_shape=[jax.ShapeDtypeStruct((rows, width), f32), jax.ShapeDtypeStruct(small.shape, f32)],
+        in_specs=[pl.BlockSpec(memory_space=pltpu.VMEM)] * 2, out_specs=[pl.BlockSpec(memory_space=pltpu.VMEM)] * 2,
+        scratch_shapes=[
+            pltpu.VMEM((chips, rows, width), bf16), pltpu.VMEM((half, 2, rows, width), bf16), pltpu.VMEM((half, 2, rows, width), bf16),
+            pltpu.VMEM((rows, padded), bf16), pltpu.VMEM((replicas, rows, padded // replicas), bf16), pltpu.VMEM((rows, padded // replicas), bf16),
+            pltpu.VMEM((rows, padded), bf16), pltpu.VMEM((n,) + small.shape, f32), pltpu.VMEM((replicas,) + small.shape, f32),
+            dma((count, chips)), dma((count, chips)), dma((count, half, 2)), dma((count, half, 2)),
+            dma((count, replicas)), dma((count, replicas)), dma((count, replicas)), dma((count, replicas)), dma((2, n)), dma((2, replicas)),
+        ],
+        compiler_params=pltpu.CompilerParams(collective_id=collective_id, has_side_effects=True, vmem_limit_bytes=48 * 2**20),
+        name="reduce_last",
+    )(grad, small)
+
+
 def twice(v):
     return jnp.pad(jnp.concatenate([jnp.pad(v, (0, DUP - NH)), v]), (0, LANE - DUP - NH))
 
@@ -386,8 +614,14 @@
     slot_count = tokens.shape[2]
     chunks = slot_count // CH
     token_count = MICRO * slot_count
-    full_in = [lax.all_gather(w_in[l], "shard", axis=0, tiled=True) for l in range(LAYERS)]
-    full_out = [lax.all_gather(w_out[l], "shard", axis=0, tiled=True) for l in range(LAYERS)]
+    replicas = lax.axis_size("replica")
+    first_in, first_out = gather([w_in[0], w_out[0]], shard_count, 1)
+    full_in, full_out = [first_in], [first_out]
+    for l in range(1, LAYERS):
+        part_in, part_out, first_in = lax.optimization_barrier((w_in[l], w_out[l], first_in))
+        full_in.append(lax.all_gather(part_in, "shard", axis=0, tiled=True))
+        full_out.append(lax.all_gather(part_out, "shard", axis=0, tiled=True))
+    full_in[0] = first_in
     global_rows = jnp.arange(MICRO) * row_total + row_index
     sequence = jnp.sum(jnp.where(jnp.arange(dealing.shape[0])[None] == global_rows[:, None], dealing[None], 0), axis=1)
     seq_length = jnp.sum(jnp.where(jnp.arange(lengths.shape[0])[None] == sequence[:, None], lengths[None], 0), axis=1)
@@ -415,22 +649,26 @@
         out_grads[l] = lax.psum_scatter(t_mm(mixed, branch_grad).astype(bf16), "shard", scatter_dimension=0, tiled=True)
         mixed_grad = mm_t(branch_grad, full_out[l]).astype(bf16)
         project_grad, sums[l] = mixer_backward(projected, scanned, states, mixed_grad, tables, chunks)
-        in_grads[l] = lax.psum_scatter(t_mm(normed, project_grad).astype(bf16), "shard", scatter_dimension=0, tiled=True)
+        in_grads[l] = t_mm(normed, project_grad).astype(bf16)
+        if l > 0:
+            in_grads[l] = lax.psum_scatter(in_grads[l], "shard", scatter_dimension=0, tiled=True)
         normed_grad = mm_t(project_grad, full_in[l])
         scale = norm_parts(entered)
         gain_grads[l] = jnp.sum(normed_grad * entered * scale, axis=0)
         inner = normed_grad * in_gain[l]
         pull = scale * scale * scale * jnp.mean(inner * entered, axis=-1, keepdims=True)
         upstream = upstream + scale * inner - pull * entered
-    in_total = lax.psum(jnp.stack(in_grads).astype(f32), "replica")
-    out_total = lax.psum(jnp.stack(out_grads).astype(f32), "replica")
-    small, gain_total = lax.psum((jnp.stack(sums), jnp.stack(gain_grads)), ("replica", "shard"))
+    later, out_total = lax.psum((jnp.stack(in_grads[1:]).astype(f32), jnp.stack(out_grads).astype(f32)), "replica")
+    small = jnp.stack(sums).at[:, 7, 2 * LANE : 2 * LANE + D].set(jnp.stack(gain_grads))
+    first, small = reduce_last(in_grads[0], small.reshape(LAYERS * 8, CONV_CH), shard_count, replicas, 2)
+    small = small.reshape(LAYERS, 8, CONV_CH)
+    in_total = jnp.concatenate([first[None], later])
     rate = -jnp.exp(a_log)
     shape = (MICRO, 1, slot_count, D)
     return (
         result.reshape(shape),
         upstream.reshape(shape),
-        gain_total,
+        small[:, 7, 2 * LANE : 2 * LANE + D],
         in_total,
         small[:, 0:4],
         small[:, 4],

time: 765 us -> 532 us (0.70)
  waiting for transfers between devices: 417 us -> 102 us
  Pallas kernels: 144 us -> 264 us
  blocking collectives: 39.4 us -> 0 us
    psum x2 -> x1, waiting for transfers between devices: 203 us -> 26.8 us  [shards(): lax.psum((jnp.stack(in_grads[1:]).astype(f32), jnp.stack(out_grads).astyp...]
    pallas_call x0 -> x2, Pallas kernels: none -> 119 us  [the longest x1 81.3 us: reduce_last(): pl.pallas_call(lambda *refs: reduce_kernel(n, replicas, groups, *refs), o...]
    all_gather x4 -> x2, waiting for transfers between devices: 90.5 us -> 22.2 us  [the longest x1 22.2 us: shards(): full_in.append(lax.all_gather(part_in, 'shard', axis=0, tiled=True))]
    reduce_scatter x2 -> x1, waiting for transfers between devices: 119 us -> 52.2 us  [shards(): lax.psum_scatter(in_grads[l], 'shard', scatter_dimension=0, tiled=True)]
    psum x1 -> x0, blocking collectives: 39.4 us -> none  [shards(): lax.psum((jnp.stack(sums), jnp.stack(gain_grads)), ('replica', 'shard'))]
    convert_element_type x0 -> x1, local copies, waits for them, and re-layouts: none -> 7.81 us  [shards(): in_grads[l] = t_mm(normed, project_grad).astype(bf16)]
  transfers between devices with their start and end apart: 10 -> 6, of which waited for: 8 -> 3; matrix products, arithmetic and copies ran while one was open for 14% -> 18% of each run, Pallas kernels for 9% -> 29%
where the time goes in v1:
time: 532 us; the launch traced here: 523 us
  Pallas kernels  264 us (50%)
  waiting for transfers between devices  102 us (19%)
  matrix products  98.4 us (18%)
  local copies, waits for them, and re-layouts  24.3 us (5%)
  other arithmetic  19 us (4%)
  between operations  15 us (3%)
    pallas_call x2, Pallas kernels, mixer_backward(): pl.pallas_call(backward_kernel, grid=(tokens // (chunks * CH), chunks), i...  97.9 us
    pallas_call x1, Pallas kernels, reduce_last(): pl.pallas_call(lambda *refs: reduce_kernel(n, replicas, groups, *refs), o...  81.3 us
    reduce_scatter x1, waiting for transfers between devices, shards(): lax.psum_scatter(in_grads[l], 'shard', scatter_dimension=0, tiled=True)  52.2 us
    pallas_call x2, Pallas kernels, mixer_forward(): pl.pallas_call(forward_kernel, grid=(tokens // (chunks * CH), chunks), in...  46.7 us
    pallas_call x1, Pallas kernels, gather(): pl.pallas_call(lambda *refs: gather_kernel(n, *refs), out_shape=[jax.Shap...  37.9 us
    dot_general x4, matrix products, mm_t(): lax.dot_general(a, b, (((1,), (1,)), ((), ())), preferred_element_type=f32)  33.6 us
    dot_general x4, matrix products, t_mm(): lax.dot_general(a, b, (((0,), (0,)), ((), ())), preferred_element_type=f32)  32.9 us
    dot_general x4, matrix products, mm(): return jnp.dot(a, b, preferred_element_type=f32)  31.9 us
  transfers between devices with their start and end apart: 6, of which 3 were waited for; matrix products, arithmetic and copies ran while one was open for 18% of the time, Pallas kernels for 29%

profile of v1, /device:TPU:0, one launch (start us, length us, event | category | flops | bytes accessed | tf_op | source)
XLA Modules:
  0.0 523.0 jit_solution(4565348512208084529)
XLA Ops:
  7.3 2.0 slice_bitcast_fusion.2
  9.3 2.5 slice_bitcast_fusion
  11.8 37.9 %gather_first.1 = (bf16[768,3352]{1,0:T(8,128)(2,1)}, bf16[1536,768]{1,0:T(8,128)(2,1)}) custom-call(bf16[96,3352]{1,0:T(8,128)(2,1)} %get-tuple-element.98.refs_0_, bf16[192,768]{1,0:T(8,128)(2,1)} %get-tuple-element.100.refs_1_), custom_call_target="tpu_custom_call" | custom-call | tf_op jit(solution)/shard_map/gather_first/pallas_call | solution.py:433
  53.3 11.6 %fusion.25.proj_ref.tail_ref = f32[1024,3352]{1,0:T(8,128)} fusion(bf16[1024,768]{1,0:T(8,128)(2,1)S(1)} %fusion.5, bf16[768,3352]{1,0:T(8,128)(2,1)} %get-tuple-element.41), kind=kOutput, calls=%fused_computation.104 | convolution fusion | flops 5272240128 | bytes 20451328 | tf_op jit(solution)/shard_map/dot_general | solution.py:32
  65.0 23.2 %mixer_forward.2 = (bf16[1024,1536]{1,0:T(8,128)(2,1)S(1)}, f32[1024,1536]{1,0:T(8,128)}, bf16[1024,1536]{1,0:T(8,128)(2,1)}) custom-call(f32[1024,3352]{1,0:T(8,128)} %fusion.25.proj_ref.tail_ref, f32[8,1792]{1,0:T(8,128)S(1)} %get-tuple-element.125.conv_ref, f32[8,128]{1,0:T(8,128)S(1)} %get-tuple-element.123.head_ref, ...), custom_call_target="tpu_custom_call" | custom-call | tf_op jit(solution)/shard_map/mixer_forward/pallas_call | solution.py:276
  88.2 4.4 multiply_reduce_fusion.2
  92.7 1.5 fusion.1
  94.5 6.5 %convolution_convert_fusion.3.grad_ref = bf16[1024,1536]{1,0:T(8,128)(2,1)} fusion(bf16[1024,768]{1,0:T(8,128)(2,1)} %fusion.1, bf16[1536,768]{1,0:T(8,128)(2,1)} %all-gather.5.cloned.1.call-done), kind=kOutput, calls=%fused_computation.3 | convolution fusion | flops 2417491968 | bytes 7077888 | tf_op jit(solution)/shard_map/dot_general | solution.py:36
  100.9 22.2 %all-gather.3.cloned.1.call-done = bf16[768,3352]{1,0:T(8,128)(2,1)} async-done(((bf16[96,3352]{1,0:T(8,128)(2,1)}), bf16[768,3352]{1,0:T(8,128)(2,1)}) %all-gather.3.cloned.1.call-update) | async-done | bytes 5148688 | tf_op jit(solution)/shard_map/all_gather | solution.py:622
  123.2 12.2 %fusion.20.proj_ref.tail_ref = f32[1024,3352]{1,0:T(8,128)} fusion(bf16[768,3352]{1,0:T(8,128)(2,1)} %all-gather.3.cloned.1.call-done, f32[1024,768]{1,0:T(8,128)} %get-tuple-element.127, f32[768]{0:T(1024)S(1)} %get-tuple-element.94, f32[1024]{0:T(1024)S(1)} %add_rsqrt_fusion), kind=kOutput, calls=%fused_computation.99 | convolution fusion | flops 5274599424 | bytes 22031360 | tf_op jit(solution)/shard_map/dot_general | solution.py:32
  135.4 23.5 %mixer_forward.3 = (bf16[1024,1536]{1,0:T(8,128)(2,1)S(1)}, f32[1024,1536]{1,0:T(8,128)}, bf16[1024,1536]{1,0:T(8,128)(2,1)}) custom-call(f32[1024,3352]{1,0:T(8,128)} %fusion.20.proj_ref.tail_ref, f32[8,1792]{1,0:T(8,128)S(1)} %get-tuple-element.124.conv_ref, f32[8,128]{1,0:T(8,128)S(1)} %get-tuple-element.122.head_ref, ...), custom_call_target="tpu_custom_call" | custom-call | tf_op jit(solution)/shard_map/mixer_forward/pallas_call | solution.py:276
  158.8 1.7 copy-done.2
  160.6 1.9 copy-done.1
  162.4 48.8 %mixer_backward.2 = (bf16[1024,3352]{1,0:T(8,128)(2,1)}, f32[8,1792]{1,0:T(8,128)S(1)}) custom-call(f32[1024,3352]{1,0:T(8,128)} %fusion.20.proj_ref.tail_ref, f32[1024,3352]{1,0:T(8,128)} %fusion.20.proj_ref.tail_ref, f32[1024,1536]{1,0:T(8,128)} %get-tuple-element.47.scan_ref, bf16[1024,1536]{1,0:T(8,128)(2,1)S(1)} %copy-done.1, ...), custom_call_target="tpu_custom_call" | custom-call | tf_op jit(solution)/shard_map/mixer_backward/pallas_call | solution.py:315
  211.3 10.2 %multiply_reduce_fusion = (f32[768]{0:T(1024)S(1)}, f32[1024]{0:T(1024)S(1)}, f32[1024,768]{1,0:T(8,128)S(1)}) fusion(f32[1024,768]{1,0:T(8,128)S(1)} %copy-done.10, f32[1024]{0:T(1024)S(1)} %add_rsqrt_fusion, f32[768]{0:T(1024)S(1)} %get-tuple-element.94, bf16[1024,3352]{1,0:T(8,128)(2,1)} %get-tuple-element.49, ...), kind=kOutput, calls=%fused_computation.23 | convolution fusion | flops 5276956672 | bytes 18319360 | tf_op jit(solution)/shard_map/dot_general | solution.py:36
  222.7 1.6 copy-done.7
  224.4 4.2 convolution_convert_fusion.5
  228.6 6.4 %convolution_convert_fusion.4 = bf16[1536,768]{1,0:T(8,128)(2,1)} fusion(bf16[1024,1536]{1,0:T(8,128)(2,1)} %copy-done.2, bf16[1024,768]{1,0:T(8,128)(2,1)} %fusion.1), kind=kOutput, calls=%fused_computation.4 | convolution fusion | flops 2417098752 | bytes 7077888 | tf_op jit(solution)/shard_map/dot_general | solution.py:40
  235.1 11.9 %convolution_convert_fusion = bf16[768,3352]{1,0:T(8,128)(2,1)} fusion(bf16[1024,3352]{1,0:T(8,128)(2,1)} %get-tuple-element.49, f32[1024,768]{1,0:T(8,128)} %get-tuple-element.127, f32[768]{0:T(1024)S(1)} %get-tuple-element.94, f32[1024]{0:T(1024)S(1)} %add_rsqrt_fusion), kind=kOutput, calls=%fused_computation | convolution fusion | flops 5277173760 | bytes 15166464 | tf_op jit(solution)/shard_map/dot_general | solution.py:40
  247.1 7.0 %convolution_convert_fusion.2.grad_ref = bf16[1024,1536]{1,0:T(8,128)(2,1)} fusion(bf16[1536,768]{1,0:T(8,128)(2,1)} %get-tuple-element.43, f32[1024,768]{1,0:T(8,128)} %copy-done.7), kind=kOutput, calls=%fused_computation.2 | convolution fusion | flops 2418278400 | bytes 8650752 | tf_op jit(solution)/shard_map/dot_general | solution.py:36
  254.1 49.1 %mixer_backward.3 = (bf16[1024,3352]{1,0:T(8,128)(2,1)}, f32[8,1792]{1,0:T(8,128)S(1)}) custom-call(f32[1024,3352]{1,0:T(8,128)} %fusion.25.proj_ref.tail_ref, f32[1024,3352]{1,0:T(8,128)} %fusion.25.proj_ref.tail_ref, f32[1024,1536]{1,0:T(8,128)} %get-tuple-element.50.scan_ref, bf16[1024,1536]{1,0:T(8,128)(2,1)S(1)} %copy-done, ...), custom_call_target="tpu_custom_call" | custom-call | tf_op jit(solution)/shard_map/mixer_backward/pallas_call | solution.py:315
  303.3 9.9 %fusion.9 = (f32[768]{0:T(1024)S(1)}, f32[1024]{0:T(1024)S(1)}, f32[1024,768]{1,0:T(8,128)}) fusion(bf16[2,1,512,768]{3,2,1,0:T(8,128)(2,1)S(1)} %copy-done.6, f32[1024]{0:T(1024)S(1)} %bitcast.128, f32[768]{0:T(1024)S(1)} %get-tuple-element.95, bf16[1024,3352]{1,0:T(8,128)(2,1)} %get-tuple-element.52, bf16[768,3352]{1,0:T(8,128)(2,1)S(1)} %bitcast.140), kind=kOutput, calls=%fused_computation.22 | convolution fusion | flops 5277743104 | bytes 16746496 | tf_op jit(solution)/shard_map/dot_general | solution.py:36
  313.2 10.5 %convolution_convert_fusion.1 = bf16[768,3352]{0,1:T(8,128)(2,1)} fusion(bf16[1024,768]{1,0:T(8,128)(2,1)S(1)} %copy-done.13, bf16[1024,3352]{1,0:T(8,128)(2,1)S(1)} %copy-done.22), kind=kOutput, calls=%fused_computation.1 | convolution fusion | flops 5274814464 | bytes 13586432 | tf_op jit(solution)/shard_map/dot_general | solution.py:40
  323.7 2.1 maximum_convert_fusion
  325.8 52.2 %reduce-scatter.4.cloned.1.call-done = bf16[96,3352]{1,0:T(8,128)(2,1)} async-done(((bf16[768,3352]{1,0:T(8,128)(2,1)}), bf16[96,3352]{1,0:T(8,128)(2,1)}) %reduce-scatter.4.cloned.1.call-update) | async-done | bytes 643600 | tf_op jit(solution)/shard_map/reduce_scatter | solution.py:654
  378.0 2.2 bitcast_convert_fusion
  380.3 7.8 %copy.52.refs_0_ = bf16[768,3352]{1,0:T(8,128)(2,1)} copy(bf16[768,3352]{0,1:T(8,128)(2,1)} %convolution_convert_fusion.1) | data formatting | bytes 10297344 | tf_op jit(solution)/shard_map/convert_element_type | solution.py:652
  388.8 81.3 %reduce_last.1 = (f32[96,3352]{1,0:T(8,128)S(1)}, f32[16,1792]{1,0:T(8,128)S(1)}) custom-call(bf16[768,3352]{1,0:T(8,128)(2,1)} %copy.52.refs_0_, f32[16,1792]{1,0:T(8,128)S(1)} %bitcast.116), custom_call_target="tpu_custom_call" | custom-call | tf_op jit(solution)/shard_map/reduce_last/pallas_call | solution.py:571
  474.5 5.4 %fusion.7 = f32[1024,768]{1,0:T(8,128)} fusion(bf16[2,1,512,768]{3,2,1,0:T(8,128)(2,1)S(1)} %copy-done.6, f32[1024,768]{1,0:T(8,128)} %copy-done.7, f32[1024,768]{1,0:T(8,128)} %get-tuple-element.129, f32[1024]{0:T(1024)S(1)} %fusion.16, f32[768]{0:T(1024)S(1)} %get-tuple-element.95, f32[1024]{0:T(1024)S(1)} %bitcast.130), kind=kLoop, calls=%fused_computation.20 | loop fusion | flops 4718592 | bytes 11021312 | tf_op jit(solution)/shard_map/sub | solution.py:660
  481.1 3.7 multiply_convert_fusion
  484.8 26.8 %all-reduce.15.cloned.1.call-done = (f32[1,96,3352]{2,1,0:T(8,128)}, f32[2,192,768]{2,1,0:T(8,128)}) async-done(((f32[1,96,3352]{2,1,0:T(8,128)}, f32[2,192,768]{2,1,0:T(8,128)}), (f32[1,96,3352]{2,1,0:T(8,128)}, f32[2,192,768]{2,1,0:T(8,128)})) %all-reduce.15.cloned.1.call-update) | async-done | bytes 2466832 | tf_op jit(solution)/shard_map/psum | solution.py:661
  511.6 3.1 pad_maximum_fusion
  (137 shorter events, 12.5 us)
Async XLA Ops:
  7.2 43.7 %copy-start.20 = (f32[2,24]{1,0:T(2,128)S(1)}, f32[2,24]{1,0:T(2,128)}, u32[]{:S(2)}) copy-start(f32[2,24]{1,0:T(2,128)} %param.25) | copy-start | bytes 580
  7.2 43.7 %copy-start.25 = (s32[64]{0:T(128)S(1)}, s32[64]{0:T(128)}, u32[]{:S(2)}) copy-start(s32[64]{0:T(128)} %param.18) | copy-start | bytes 772
  7.2 43.8 %copy-start.26 = (s32[64]{0:T(128)S(1)}, s32[64]{0:T(128)}, u32[]{:S(2)}) copy-start(s32[64]{0:T(128)} %param.17) | copy-start | bytes 772
  7.2 44.1 %copy-start.6 = (bf16[2,1,512,768]{3,2,1,0:T(8,128)(2,1)S(1)}, bf16[2,1,512,768]{3,2,1,0:T(8,128)(2,1)}, u32[]{:S(2)}) copy-start(bf16[2,1,512,768]{3,2,1,0:T(8,128)(2,1)} %param.15) | copy-start | bytes 4718596
  7.2 87.2 %all-gather.5.cloned.1.call-start = ((), (), s32[]{:S(2)}) async-start(), calls=%async_computation.4 | async-start | bytes 2654208 | tf_op jit(solution)/shard_map/all_gather | solution.py:623
  9.3 42.7 %copy-start.21 = (f32[2,24]{1,0:T(2,128)S(1)}, f32[2,24]{1,0:T(2,128)}, u32[]{:S(2)}) copy-start(f32[2,24]{1,0:T(2,128)} %param.23) | copy-start | bytes 580
  9.3 42.8 %copy-start.18 = (f32[2,24]{1,0:T(2,128)S(1)}, f32[2,24]{1,0:T(2,128)}, u32[]{:S(2)}) copy-start(f32[2,24]{1,0:T(2,128)} %param.24) | copy-start | bytes 580
  9.3 43.1 %copy-start.19 = (f32[2,768]{1,0:T(2,128)S(1)}, f32[2,768]{1,0:T(2,128)}, u32[]{:S(2)}) copy-start(f32[2,768]{1,0:T(2,128)} %param.19) | copy-start | bytes 18436
  49.7 3.2 copy-start.17
  49.7 3.2 copy-start.16
  49.7 3.3 copy-start.15
  49.7 73.4 %all-gather.3.cloned.1.call-start = ((), (), s32[]{:S(2)}) async-start(), calls=%async_computation.3 | async-start | bytes 5971968 | tf_op jit(solution)/shard_map/all_gather | solution.py:622
  50.5 273.2 %reduce-scatter.6.cloned.1.call-start = ((), (), s32[]{:S(2)}) async-start(), calls=%async_computation.6 | async-start | bytes 2654208 | tf_op jit(solution)/shard_map/reduce_scatter | solution.py:649
  52.9 12.1 %copy-start.12 = (bf16[1024,768]{1,0:T(8,128)(2,1)}, bf16[1024,768]{1,0:T(8,128)(2,1)S(1)}, u32[]{:S(2)}) copy-start(bf16[1024,768]{1,0:T(8,128)(2,1)S(1)} %fusion.5) | copy-start | bytes 4718596
  65.0 23.2 %copy-start.24 = (bf16[1536,768]{1,0:T(8,128)(2,1)S(1)}, bf16[1536,768]{1,0:T(8,128)(2,1)}, u32[]{:S(2)}) copy-start(bf16[1536,768]{1,0:T(8,128)(2,1)} %get-tuple-element.43) | copy-start | bytes 7077892
  88.2 4.4 copy-start.4
  88.2 4.4 copy-start.8
  162.4 48.8 %copy-start.10 = (f32[1024,768]{1,0:T(8,128)S(1)}, f32[1024,768]{1,0:T(8,128)}, u32[]{:S(2)}) copy-start(f32[1024,768]{1,0:T(8,128)} %get-tuple-element.127) | copy-start | bytes 9437188
  211.3 10.2 %copy-start.9 = (bf16[2,1,512,768]{3,2,1,0:T(8,128)(2,1)S(1)}, bf16[2,1,512,768]{3,2,1,0:T(8,128)(2,1)}, u32[]{:S(2)}) copy-start(bf16[2,1,512,768]{3,2,1,0:T(8,128)(2,1)} %param.16) | copy-start | bytes 4718596
  221.5 2.8 copy-start.5
  228.5 95.1 %reduce-scatter.8.cloned.1.call-start = ((), (), s32[]{:S(2)}) async-start(), calls=%async_computation.7 | async-start | bytes 2654208 | tf_op jit(solution)/shard_map/reduce_scatter | solution.py:649
  235.0 143.0 %reduce-scatter.4.cloned.1.call-start = ((), (), s32[]{:S(2)}) async-start(), calls=%async_computation.5 | async-start | bytes 5971968 | tf_op jit(solution)/shard_map/reduce_scatter | solution.py:654
  247.0 264.6 %all-reduce.15.cloned.1.call-start = ((), (), s32[]{:S(2)}) async-start(), calls=%async_computation.8 | async-start | bytes 5013504 | tf_op jit(solution)/shard_map/psum | solution.py:661
  247.1 7.1 %copy-start = (bf16[1024,1536]{1,0:T(8,128)(2,1)S(1)}, bf16[1024,1536]{1,0:T(8,128)(2,1)}, u32[]{:S(2)}) copy-start(bf16[1024,1536]{1,0:T(8,128)(2,1)} %get-tuple-element.51.saved_ref) | copy-start | bytes 9437188
  247.1 56.2 %slice-start = ((s8[5308416]{0:T(1024)(128)(4,1)}), s8[4194304]{0:T(1024)(128)(4,1)S(1)}, s32[]{:S(2)}) async-start(s8[5308416]{0:T(1024)(128)(4,1)} %bitcast.139), calls=%async_computation.9 | async-start | bytes 8388608
  254.1 49.1 %slice-start.1 = ((s8[5308416]{0:T(1024)(128)(4,1)}), s8[1114112]{0:T(1024)(128)(4,1)S(1)}, s32[]{:S(2)}) async-start(s8[5308416]{0:T(1024)(128)(4,1)} %bitcast.139), calls=%async_computation.10 | async-start | bytes 2228224
  303.3 9.9 %copy-start.13 = (bf16[1024,768]{1,0:T(8,128)(2,1)S(1)}, bf16[1024,768]{1,0:T(8,128)(2,1)}, u32[]{:S(2)}) copy-start(bf16[1024,768]{1,0:T(8,128)(2,1)} %copy-done.12) | copy-start | bytes 4718596
  303.3 9.9 %copy-start.22 = (bf16[1024,3352]{1,0:T(8,128)(2,1)S(1)}, bf16[1024,3352]{1,0:T(8,128)(2,1)}, u32[]{:S(2)}) copy-start(bf16[1024,3352]{1,0:T(8,128)(2,1)} %get-tuple-element.52) | copy-start | bytes 20594692
  474.5 5.4 %copy-start.3 = (bf16[1024,1536]{1,0:T(8,128)(2,1)S(1)}, bf16[1024,1536]{1,0:T(8,128)(2,1)}, u32[]{:S(2)}) copy-start(bf16[1024,1536]{1,0:T(8,128)(2,1)} %copy-done.2) | copy-start | bytes 9437188
  474.5 5.4 %copy-start.11 = (f32[1024,768]{1,0:T(8,128)S(1)}, f32[1024,768]{1,0:T(8,128)}, u32[]{:S(2)}) copy-start(f32[1024,768]{1,0:T(8,128)} %get-tuple-element.127) | copy-start | bytes 9437188
  474.5 6.6 %copy-start.23 = (bf16[1536,768]{1,0:T(8,128)(2,1)S(1)}, bf16[1536,768]{1,0:T(8,128)(2,1)}, u32[]{:S(2)}) copy-start(bf16[1536,768]{1,0:T(8,128)(2,1)} %all-gather.5.cloned.1.call-done) | copy-start | bytes 7077892
  511.6 3.1 copy-start.14
  (3 other events, 5.3 us)
Sparse Core Ops, SparseCore 0:
  49.9 29.3 all-gather.4
  81.7 41.3 all-gather.2
  228.7 42.4 reduce-scatter.5
  275.3 42.4 reduce-scatter.7
  321.1 56.8 reduce-scatter.3
  381.6 129.9 all-reduce.14

commit v2 on v0

--- a/solution.py
+++ b/solution.py
@@ -25,6 +25,7 @@
 f32 = jnp.float32
 bf16 = jnp.bfloat16
 highest = lax.Precision.HIGHEST
+MESH = pl.DeviceIdType.MESH
 
 
 def mm(a, b):
@@ -264,57 +265,479 @@
     dconv_ref[CH : CH + 8] = dconv_ref[0:8]
 
 
+def ring_place(n):
+    wide = n // 4
+    me = lax.axis_index("shard")
+    chip, core = me // 2, me % 2
+    row, col = chip // wide, chip % wide
+    place = row * (2 * wide - 1 - col) + (1 - row) * col
+
+    def shard_of(at, c):
+        at = at % (2 * wide)
+        r = at // wide
+        x = r * (2 * wide - 1 - at) + (1 - r) * at
+        return (r * wide + x) * 2 + c
+
+    return place, core, shard_of
+
+
+def halves(rows):
+    first = rows // 2 // 16 * 16
+    return (0, first), (first, rows - first)
+
+
+def aligned(start, size, unit=16):
+    return pl.ds(pl.multiple_of(start, unit), size)
+
+
+def column_groups(width, replicas, parts):
+    unit = LANE * replicas
+    units = -(-width // unit)
+    parts = min(parts, units)
+    groups, start = [], 0
+    for g in range(parts):
+        size = (units // parts + (g < units % parts)) * unit
+        groups.append((start, size, min(size, width - start)))
+        start += size
+    return groups, start
+
+
+def remote(src, dst, send, recv, axis, to):
+    return pltpu.make_async_remote_copy(
+        src_ref=src, dst_ref=dst, send_sem=send, recv_sem=recv, device_id={axis: to}, device_id_type=MESH
+    )
+
+
+class Gather:
+    def __init__(self, n, parts):
+        self.n, self.half = n, n // 4
+        self.shapes = [p.shape for p in parts]
+        self.dtypes = [p.dtype for p in parts]
+        self.stage_count = self.half + 2
+
+    def in_count(self):
+        return len(self.shapes)
+
+    def out_count(self):
+        return len(self.shapes)
+
+    def in_specs(self):
+        return [pl.BlockSpec(memory_space=pl.ANY)] * len(self.shapes)
+
+    out_specs = in_specs
+
+    def out_shapes(self):
+        return [jax.ShapeDtypeStruct((r * self.n, w), t) for (r, w), t in zip(self.shapes, self.dtypes)]
+
+    def scratch(self):
+        count = len(self.shapes)
+        dma = pltpu.SemaphoreType.DMA
+        return [
+            dma((count, self.half, 2)), dma((count, self.half, 2)),
+            dma((count, self.half + 1, 2)), dma((count, self.half + 1, 2)), dma((count,)),
+        ]
+
+    def stages(self, parts, wholes, scratch):
+        ring_send, ring_recv, pair_send, pair_recv, own_sem = scratch
+        n, half = self.n, self.half
+        place, core, shard_of = ring_place(n)
+        right, left, pair = shard_of(place + 1, core), shard_of(place + n // 2 - 1, core), shard_of(place, 1 - core)
+        me = shard_of(place, core)
+        arrays = range(len(self.shapes))
+        ways = ((0, right), (1, left))
+
+        def rows_of(a, s, d):
+            rows = self.shapes[a][0]
+            return (0, rows) if s < half else halves(rows)[d]
+
+        def span(a, owner, part):
+            return aligned(owner * self.shapes[a][0] + part[0], part[1])
+
+        def hop(a, s, d, to):
+            owner = shard_of(place + (n // 2 - (s - 1) if d == 0 else s - 1), core)
+            part = rows_of(a, s, d)
+            src = parts[a].at[aligned(part[0], part[1])] if s == 1 else wholes[a].at[span(a, owner, part)]
+            return remote(src, wholes[a].at[span(a, owner, part)], ring_send.at[a, s - 1, d], ring_recv.at[a, s - 1, d], "shard", to)
+
+        def cross(a, s, d):
+            owner = me if s == 0 else shard_of(place + (n // 2 - s if d == 0 else s), core)
+            part = (0, self.shapes[a][0]) if s == 0 else rows_of(a, s, d)
+            src = parts[a] if s == 0 else wholes[a].at[span(a, owner, part)]
+            return remote(src, wholes[a].at[span(a, owner, part)], pair_send.at[a, s, d], pair_recv.at[a, s, d], "shard", pair)
+
+        def own(a):
+            return pltpu.make_async_copy(parts[a], wholes[a].at[span(a, me, (0, self.shapes[a][0]))], own_sem.at[a])
+
+        crossings = [(0, 0)] + [(s, d) for s in range(1, half + 1) for d in (0, 1)]
+
+        def first():
+            barrier = pltpu.get_barrier_semaphore()
+            for to in (right, left, pair):
+                pl.semaphore_signal(barrier, inc=1, device_id={"shard": to}, device_id_type=MESH)
+            pl.semaphore_wait(barrier, 3)
+            for a in arrays:
+                for d, to in ways:
+                    hop(a, 1, d, to).start()
+                cross(a, 0, 0).start()
+                own(a).start()
+
+        def forward(s):
+            for a in arrays:
+                for d, to in ways:
+                    hop(a, s, d, to).wait_recv()
+                    if s < half:
+                        hop(a, s + 1, d, to).start()
+                    cross(a, s, d).start()
+
+        def last():
+            for a in arrays:
+                for s, d in crossings:
+                    cross(a, s, d).wait_recv()
+                for s, d in crossings:
+                    cross(a, s, d).wait_send()
+                for s in range(1, half + 1):
+                    for d, to in ways:
+                        hop(a, s, d, to).wait_send()
+                own(a).wait()
+
+        return [first] + [lambda s=s: forward(s) for s in range(1, half + 1)] + [last]
+
+
+class Reduce:
+    def __init__(self, n, replicas, grads, groups, small=None):
+        self.n, self.replicas = n, replicas
+        self.chips, self.half = n // 2, n // 4
+        self.shapes = [(g.shape[0] // n, g.shape[1]) for g in grads]
+        self.groups = [column_groups(w, replicas, count) for (_, w), count in zip(self.shapes, groups)]
+        self.small = small
+        self.stage_count = self.half + 4
+
+    def in_count(self):
+        return len(self.shapes) + (self.small is not None)
+
+    out_count = in_count
+
+    def in_specs(self):
+        specs = [pl.BlockSpec(memory_space=pl.ANY)] * len(self.shapes)
+        return specs + ([pl.BlockSpec(memory_space=pltpu.VMEM)] if self.small is not None else [])
+
+    def out_specs(self):
+        specs = [pl.BlockSpec(memory_space=pl.ANY)] * len(self.shapes)
+        return specs + ([pl.BlockSpec(memory_space=pltpu.VMEM)] if self.small is not None else [])
+
+    def out_shapes(self):
+        shapes = [jax.ShapeDtypeStruct(s, f32) for s in self.shapes]
+        return shapes + ([jax.ShapeDtypeStruct(self.small.shape, f32)] if self.small is not None else [])
+
+    def scratch(self):
+        dma = pltpu.SemaphoreType.DMA
+        items = []
+        for (rows, width), (groups, padded) in zip(self.shapes, self.groups):
+            g, each = len(groups), padded // self.replicas
+            items += [
+                pltpu.VMEM((self.chips, rows, width), bf16),
+                pltpu.VMEM((self.chips, rows, width), bf16),
+                pltpu.VMEM((self.half, 2, rows, width), bf16),
+                pltpu.VMEM((self.half, 2, rows, width), bf16),
+                pltpu.VMEM((rows, padded), bf16),
+                pltpu.VMEM((self.replicas, rows, each), bf16),
+                pltpu.VMEM((rows, each), bf16),
+                pltpu.VMEM((rows, padded), bf16),
+                pltpu.VMEM((rows, width), f32),
+                dma((g, self.chips, 3)), dma((g, self.half, 2, 2)), dma((g, self.replicas, 4)), dma((1,)),
+            ]
+        if self.small is not None:
+            items += [
+                pltpu.VMEM((self.n,) + self.small.shape, f32),
+                pltpu.VMEM((self.replicas,) + self.small.shape, f32),
+                dma((2, self.n)), dma((2, self.replicas)),
+            ]
+        return items
+
+    def stages(self, ins, outs, scratch):
+        n, replicas, chips, half = self.n, self.replicas, self.chips, self.half
+        place, core, shard_of = ring_place(n)
+        right, left, pair = shard_of(place + 1, core), shard_of(place + chips - 1, core), shard_of(place, 1 - core)
+        me, mine = lax.axis_index("shard"), lax.axis_index("replica")
+        ways = ((0, right), (1, left))
+        order = [half] + [v for s in range(half - 1, 0, -1) for v in (s, chips - s)] + [0]
+        work = [(a, g) for a in range(len(self.shapes)) for g in range(len(self.groups[a][0]))]
+        buffers = [scratch[13 * a : 13 * a + 13] for a in range(len(self.shapes))]
+        if self.small is not None:
+            small_ref, total_ref = ins[-1], outs[-1]
+            small_buf, small_cross, small_sem, cross_sem = scratch[13 * len(self.shapes) :]
+
+        def cols_of(a, g):
+            start, _, wide = self.groups[a][0][g]
+            return slice(start, start + wide)
+
+        def piece(a, g, owner):
+            rows = self.shapes[a][0]
+            return ins[a].at[aligned(owner * rows, rows), cols_of(a, g)]
+
+        def pairing(a, g, q):
+            sem = buffers[a][9]
+            return remote(piece(a, g, shard_of(place + q, 1 - core)), buffers[a][1].at[q, :, cols_of(a, g)],
+                          sem.at[g, q, 0], sem.at[g, q, 1], "shard", pair)
+
+        def loading(a, g, q):
+            return pltpu.make_async_copy(piece(a, g, shard_of(place + q, core)), buffers[a][0].at[q, :, cols_of(a, g)], buffers[a][9].at[g, q, 2])
+
+        def part_of(a, k, d):
+            rows = self.shapes[a][0]
+            return halves(rows)[d] if k == 1 else (0, rows)
+
+        def ringing(a, g, k, d, to):
+            first, count = part_of(a, k, d)
+            sem = buffers[a][10]
+            return remote(buffers[a][2].at[k - 1, d, first : first + count, cols_of(a, g)],
+                          buffers[a][3].at[k - 1, d, first : first + count, cols_of(a, g)],
+                          sem.at[g, k - 1, d, 0], sem.at[g, k - 1, d, 1], "shard", to)
+
+        def block(a, g, index):
+            start, size, _ = self.groups[a][0][g]
+            return aligned(start + index * (size // replicas), size // replicas, LANE)
+
+        def slot(a, g):
+            start, size, _ = self.groups[a][0][g]
+            return slice(start // replicas, (start + size) // replicas)
+
+        def crossing(a, g, s):
+            to = (mine + s) % replicas
+            sem = buffers[a][11]
+            return remote(buffers[a][4].at[:, block(a, g, to)], buffers[a][5].at[s, :, slot(a, g)],
+                          sem.at[g, s, 0], sem.at[g, s, 1], "replica", to)
+
+        def sharing(a, g, s):
+            to = (mine + s) % replicas
+            sem = buffers[a][11]
+            return remote(buffers[a][6].at[:, slot(a, g)], buffers[a][7].at[:, block(a, g, mine)],
+                          sem.at[g, s, 2], sem.at[g, s, 3], "replica", to)
+
+        def storing(a):
+            return pltpu.make_async_copy(buffers[a][8], outs[a], buffers[a][12].at[0])
+
+        def small_plane(s):
+            return remote(small_ref, small_buf.at[s], small_sem.at[0, s], small_sem.at[1, s], "shard", (me + s) % n)
+
+        def small_across(s):
+            return remote(small_cross.at[0], small_cross.at[s], cross_sem.at[0, s], cross_sem.at[1, s], "replica", (mine + s) % replicas)
+
+        def both(a, g, q, part):
+            first, count = part
+            rows, cols = slice(first, first + count), cols_of(a, g)
+            return buffers[a][0][q, rows, cols].astype(f32) + buffers[a][1][q, rows, cols].astype(f32)
+
+        def arrived(a, g, q):
+            loading(a, g, q).wait()
+            pairing(a, g, q).wait_recv()
+
+        def first():
+            barrier = pltpu.get_barrier_semaphore()
+            near = [(me + s) % n for s in range(1, n)] if self.small is not None else [right, left, pair]
+            for to in near:
+                pl.semaphore_signal(barrier, inc=1, device_id={"shard": to}, device_id_type=MESH)
+            for s in range(1, replicas):
+                pl.semaphore_signal(barrier, inc=1, device_id={"replica": (mine + s) % replicas}, device_id_type=MESH)
+            pl.semaphore_wait(barrier, len(near) + replicas - 1)
+            for i, (a, g) in enumerate(work):
+                for q in order:
+                    pairing(a, g, q).start()
+                    loading(a, g, q).start()
+                if i == 0 and self.small is not None:
+                    for s in range(1, n):
+                        small_plane(s).start()
+
+        def turn(k):
+            for a, g in work:
+                cols = cols_of(a, g)
+                for d, to in ways:
+                    q = half - k + 1 if d == 0 else chips - (half - k + 1)
+                    if k > 1 or d == 0:
+                        arrived(a, g, q)
+                    if k > 1:
+                        ringing(a, g, k - 1, d, to).wait_recv()
+                    pieces = [part_of(a, 1, d)] if k == 1 else halves(self.shapes[a][0]) if k == 2 else [part_of(a, k, d)]
+                    for e, (at, many) in enumerate(pieces):
+                        value = both(a, g, q, (at, many))
+                        if k > 2 or (k == 2 and e == d):
+                            value = value + buffers[a][3][k - 2, d, at : at + many, cols].astype(f32)
+                        buffers[a][2][k - 1, d, at : at + many, cols] = value.astype(bf16)
+                    ringing(a, g, k, d, to).start()
+            if k == 1 and self.small is not None:
+                for s in range(1, n):
+                    small_plane(s).wait_recv()
+                small_buf[0] = small_ref[...]
+                small_cross[0] = lax.fori_loop(
+                    0, n, lambda i, acc: acc + small_buf[(me - i + n) % n], jnp.zeros(self.small.shape, f32)
+                )
+                for s in range(1, replicas):
+                    small_across(s).start()
+
+        def settle():
+            for a, g in work:
+                cols = cols_of(a, g)
+                start, size, wide = self.groups[a][0][g]
+                rows = self.shapes[a][0]
+                arrived(a, g, 0)
+                value = both(a, g, 0, (0, rows))
+                for d, to in ways:
+                    ringing(a, g, half, d, to).wait_recv()
+                    value = value + buffers[a][3][half - 1, d, :, cols].astype(f32)
+                buffers[a][4][:, cols] = value.astype(bf16)
+                if wide < size:
+                    buffers[a][4][:, start + wide : start + size] = jnp.zeros((rows, size - wide), bf16)
+                for s in range(1, replicas):
+                    crossing(a, g, s).start()
+
+        def share():
+            for a, g in work:
+                cols = slot(a, g)
+                for s in range(1, replicas):
+                    crossing(a, g, s).wait_recv()
+                value = buffers[a][4][:, block(a, g, mine)].astype(f32)
+                for s in range(1, replicas):
+                    value = value + buffers[a][5][s, :, cols].astype(f32)
+                buffers[a][6][:, cols] = value.astype(bf16)
+                for s in range(1, replicas):
+                    sharing(a, g, s).start()
+                buffers[a][7][:, block(a, g, mine)] = value.astype(bf16)
+
+        def last():
+            if self.small is not None:
+                for s in range(1, replicas):
+                    small_across(s).wait_recv()
+                total_ref[...] = lax.fori_loop(
+                    0, replicas, lambda i, acc: acc + small_cross[(mine - i + replicas) % replicas],
+                    jnp.zeros(self.small.shape, f32),
+                )
+            for a, g in work:
+                cols = cols_of(a, g)
+                for s in range(1, replicas):
+                    sharing(a, g, s).wait_recv()
+                buffers[a][8][:, cols] = buffers[a][7][:, cols].astype(f32)
+            for a in range(len(self.shapes)):
+                storing(a).start()
+            for a, g in work:
+                for q in order:
+                    pairing(a, g, q).wait_send()
+                for k in range(1, half + 1):
+                    for d, to in ways:
+                        ringing(a, g, k, d, to).wait_send()
+                for s in range(1, replicas):
+                    crossing(a, g, s).wait_send()
+                    sharing(a, g, s).wait_send()
+            if self.small is not None:
+                for s in range(1, n):
+                    small_plane(s).wait_send()
+                for s in range(1, replicas):
+                    small_across(s).wait_send()
+            for a in range(len(self.shapes)):
+                storing(a).wait()
+
+        return [first] + [lambda k=k: turn(k) for k in range(1, half + 1)] + [settle, share, last]
+
+
+def move(engine, operands, collective_id, name):
+    def kernel(*refs):
+        i, o = engine.in_count(), engine.out_count()
+        for stage in engine.stages(refs[:i], refs[i : i + o], refs[i + o :]):
+            stage()
+
+    return pl.pallas_call(
+        kernel,
+        out_shape=engine.out_shapes(),
+        in_specs=engine.in_specs(),
+        out_specs=engine.out_specs(),
+        scratch_shapes=engine.scratch(),
+        compiler_params=pltpu.CompilerParams(
+            collective_id=collective_id, has_side_effects=True, vmem_limit_bytes=56 * 2**20
+        ),
+        name=name,
+    )(*operands)
+
+
+def beside(body, counts, engine, steps, total):
+    ins, outs, scratch = counts
+
+    def kernel(*refs):
+        i, o = engine.in_count(), engine.out_count()
+        own_in, refs = refs[:ins], refs[ins:]
+        far_in, refs = refs[:i], refs[i:]
+        own_out, refs = refs[:outs], refs[outs:]
+        far_out, refs = refs[:o], refs[o:]
+        own_scratch, far_scratch = refs[:scratch], refs[scratch:]
+        stages = engine.stages(far_in, far_out, far_scratch)
+        step = pl.program_id(0) * pl.num_programs(1) + pl.program_id(1)
+        for at, stage in zip(steps, stages[:-1]):
+            pl.when(step == at)(stage)
+        body(*own_in, *own_out, *own_scratch)
+        pl.when(step == total - 1)(stages[-1])
+
+    return kernel
+
+
 def fixed(shape):
     return pl.BlockSpec(shape, lambda r, c: (0,) * len(shape))
 
 
-def mixer_forward(projected, tables, chunks):
+def grid_call(body, grid, operands, in_specs, out_specs, out_shapes, scratch, name, limit, extra):
+    if extra is None:
+        return pl.pallas_call(
+            body, grid=grid, in_specs=in_specs, out_specs=out_specs, out_shape=out_shapes, scratch_shapes=scratch,
+            compiler_params=pltpu.CompilerParams(dimension_semantics=("arbitrary", "arbitrary"), vmem_limit_bytes=limit),
+            name=name,
+        )(*operands)
+    engine, given, steps, collective_id = extra
+    total = grid[0] * grid[1]
+    kernel = beside(body, (len(in_specs), len(out_specs), len(scratch)), engine, [min(s, total - 1) for s in steps], total)
+    return pl.pallas_call(
+        kernel, grid=grid, in_specs=in_specs + engine.in_specs(), out_specs=out_specs + engine.out_specs(),
+        out_shape=out_shapes + engine.out_shapes(), scratch_shapes=scratch + engine.scratch(),
+        compiler_params=pltpu.CompilerParams(
+            dimension_semantics=("arbitrary", "arbitrary"), vmem_limit_bytes=limit,
+            collective_id=collective_id, has_side_effects=True,
+        ),
+        name=name + "_sending",
+    )(*operands, *given)
+
+
+def mixer_forward(projected, tables, chunks, extra=None):
     tokens = projected.shape[0]
     conv_t, head_t, wide_t, spread, _ = tables
     block = lambda r, c: (r * chunks + c, 0)
-    return pl.pallas_call(
+    return grid_call(
         forward_kernel,
-        grid=(tokens // (chunks * CH), chunks),
-        in_specs=[
-            pl.BlockSpec((CH, NIN), block),
-            fixed((8, CONV_CH)),
-            fixed((8, LANE)),
-            fixed((8, DI)),
-            fixed((LANE, DI)),
-        ],
-        out_specs=[
-            pl.BlockSpec((CH, DI), block),
-            pl.BlockSpec((CH, DI), block),
-            pl.BlockSpec((NSTATE, DI), block),
-        ],
-        out_shape=[
+        (tokens // (chunks * CH), chunks),
+        (projected, conv_t, head_t, wide_t, spread),
+        [pl.BlockSpec((CH, NIN), block), fixed((8, CONV_CH)), fixed((8, LANE)), fixed((8, DI)), fixed((LANE, DI))],
+        [pl.BlockSpec((CH, DI), block), pl.BlockSpec((CH, DI), block), pl.BlockSpec((NSTATE, DI), block)],
+        [
             jax.ShapeDtypeStruct((tokens, DI), bf16),
             jax.ShapeDtypeStruct((tokens, DI), f32),
             jax.ShapeDtypeStruct((tokens // CH * NSTATE, DI), bf16),
         ],
-        scratch_shapes=[
+        [
             pltpu.VMEM((CH + 8, CONV_CH), f32),
             pltpu.VMEM((CH, LANE), f32),
             pltpu.VMEM((NSTATE, DI), f32),
             pltpu.VMEM((CH, DI), f32),
             pltpu.VMEM((CH, DI), bf16),
         ],
-        compiler_params=pltpu.CompilerParams(
-            dimension_semantics=("arbitrary", "arbitrary"), vmem_limit_bytes=48 * 2**20
-        ),
-        name="mixer_forward",
-    )(projected, conv_t, head_t, wide_t, spread)
-
-
-def mixer_backward(projected, scanned, saved, mixed_grad, tables, chunks):
+        "mixer_forward", 48 * 2**20, extra,
+    )
+
+
+def mixer_backward(projected, scanned, saved, mixed_grad, tables, chunks, extra=None):
     tokens = projected.shape[0]
     conv_t, head_t, wide_t, spread, gather = tables
     block = lambda r, c: (r * chunks + chunks - 1 - c, 0)
     ahead = lambda r, c: (jnp.maximum((r * chunks + chunks - 1 - c) * (CH // 8) - 1, 0), 0)
-    return pl.pallas_call(
+    return grid_call(
         backward_kernel,
-        grid=(tokens // (chunks * CH), chunks),
-        in_specs=[
+        (tokens // (chunks * CH), chunks),
+        (projected, projected, scanned, saved, mixed_grad, conv_t, head_t, wide_t, spread, gather),
+        [
             pl.BlockSpec((CH, NIN), block),
             pl.BlockSpec((8, NIN), ahead),
             pl.BlockSpec((CH, DI), block),
@@ -326,15 +749,9 @@
             fixed((LANE, DI)),
             fixed((DI, LANE)),
         ],
-        out_specs=[
-            pl.BlockSpec((CH, NIN), block),
-            fixed((8, CONV_CH)),
-        ],
-        out_shape=[
-            jax.ShapeDtypeStruct((tokens, NIN), bf16),
-            jax.ShapeDtypeStruct((8, CONV_CH), f32),
-        ],
-        scratch_shapes=[
+        [pl.BlockSpec((CH, NIN), block), fixed((8, CONV_CH))],
+        [jax.ShapeDtypeStruct((tokens, NIN), bf16), jax.ShapeDtypeStruct((8, CONV_CH), f32)],
+        [
             pltpu.VMEM((CH + 8, CONV_CH), f32),
             pltpu.VMEM((CH, LANE), f32),
             pltpu.VMEM((NSTATE, DI), f32),
@@ -349,11 +766,8 @@
             pltpu.VMEM((CH, DI), bf16),
             pltpu.VMEM((8, DI), f32),
         ],
-        compiler_params=pltpu.CompilerParams(
-            dimension_semantics=("arbitrary", "arbitrary"), vmem_limit_bytes=48 * 2**20
-        ),
-        name="mixer_backward",
-    )(projected, projected, scanned, saved, mixed_grad, conv_t, head_t, wide_t, spread, gather)
+        "mixer_backward", 60 * 2**20, extra,
+    )
 
 
 def twice(v):
@@ -386,8 +800,10 @@
     slot_count = tokens.shape[2]
     chunks = slot_count // CH
     token_count = MICRO * slot_count
-    full_in = [lax.all_gather(w_in[l], "shard", axis=0, tiled=True) for l in range(LAYERS)]
-    full_out = [lax.all_gather(w_out[l], "shard", axis=0, tiled=True) for l in range(LAYERS)]
+    replicas = lax.axis_size("replica")
+    engine = Gather(shard_count, [w_in[0], w_out[0]])
+    first_in, first_out = move(engine, (w_in[0], w_out[0]), 1, "gather_first")
+    full_in, full_out = [first_in, None], [first_out, None]
     global_rows = jnp.arange(MICRO) * row_total + row_index
     sequence = jnp.sum(jnp.where(jnp.arange(dealing.shape[0])[None] == global_rows[:, None], dealing[None], 0), axis=1)
     seq_length = jnp.sum(jnp.where(jnp.arange(lengths.shape[0])[None] == sequence[:, None], lengths[None], 0), axis=1)
@@ -399,7 +815,13 @@
         normed = (stream * norm_parts(stream) * in_gain[l]).astype(bf16)
         projected = mm(normed, full_in[l])
         tables = mixer_tables(conv_w[l], conv_b[l], dt_bias[l], a_log[l], d_skip[l], out_gain[l])
-        mixed, scanned, states = mixer_forward(projected, tables, chunks)
+        later = w_in[1] if l == 0 else w_out[1]
+        engine = Gather(shard_count, [later])
+        mixed, scanned, states, whole = mixer_forward(projected, tables, chunks, (engine, (later,), (0, 4, 7, 7), 2 + l))
+        if l == 0:
+            full_in[1] = whole
+        else:
+            full_out[1] = whole
         saved.append((stream, normed, projected, tables, mixed, scanned, states))
         stream = stream + mm(mixed, full_out[l])
     result = (stream * valid).astype(bf16)
@@ -412,25 +834,36 @@
     for l in reversed(range(LAYERS)):
         entered, normed, projected, tables, mixed, scanned, states = saved[l]
         branch_grad = upstream.astype(bf16)
-        out_grads[l] = lax.psum_scatter(t_mm(mixed, branch_grad).astype(bf16), "shard", scatter_dimension=0, tiled=True)
+        out_grad = t_mm(mixed, branch_grad).astype(bf16)
         mixed_grad = mm_t(branch_grad, full_out[l]).astype(bf16)
-        project_grad, sums[l] = mixer_backward(projected, scanned, states, mixed_grad, tables, chunks)
-        in_grads[l] = lax.psum_scatter(t_mm(normed, project_grad).astype(bf16), "shard", scatter_dimension=0, tiled=True)
+        given = (out_grad,) if l > 0 else (in_grad, out_grad)
+        engine = Reduce(shard_count, replicas, given, [1] * len(given))
+        steps = (0, 1, 2, 3, 4, 5, 6) if l > 0 else (0, 1, 3, 6, 7, 7, 7)
+        project_grad, sums[l], *done = mixer_backward(
+            projected, scanned, states, mixed_grad, tables, chunks, (engine, given, steps, 4 + l)
+        )
+        if l > 0:
+            out_grads[1] = done[0]
+        else:
+            in_grads[1], out_grads[0] = done
+        in_grad = t_mm(normed, project_grad).astype(bf16)
         normed_grad = mm_t(project_grad, full_in[l])
         scale = norm_parts(entered)
         gain_grads[l] = jnp.sum(normed_grad * entered * scale, axis=0)
         inner = normed_grad * in_gain[l]
         pull = scale * scale * scale * jnp.mean(inner * entered, axis=-1, keepdims=True)
         upstream = upstream + scale * inner - pull * entered
-    in_total = lax.psum(jnp.stack(in_grads).astype(f32), "replica")
-    out_total = lax.psum(jnp.stack(out_grads).astype(f32), "replica")
-    small, gain_total = lax.psum((jnp.stack(sums), jnp.stack(gain_grads)), ("replica", "shard"))
+    small = jnp.stack(sums).at[:, 7, 2 * LANE : 2 * LANE + D].set(jnp.stack(gain_grads)).reshape(LAYERS * 8, CONV_CH)
+    engine = Reduce(shard_count, replicas, (in_grad,), [3], small)
+    in_grads[0], small = move(engine, (in_grad, small), 6, "reduce_last")
+    small = small.reshape(LAYERS, 8, CONV_CH)
+    in_total, out_total = jnp.stack(in_grads), jnp.stack(out_grads)
     rate = -jnp.exp(a_log)
     shape = (MICRO, 1, slot_count, D)
     return (
         result.reshape(shape),
         upstream.reshape(shape),
-        gain_total,
+        small[:, 7, 2 * LANE : 2 * LANE + D],
         in_total,
         small[:, 0:4],
         small[:, 4],

time: 765 us -> 453 us (0.59)
  waiting for transfers between devices: 417 us -> 0 us
  Pallas kernels: 144 us -> 309 us
  blocking collectives: 39.4 us -> 0 us
  between operations: 14.8 us -> 1.41 us
  matrix products: 101 us -> 88.8 us
    psum x2 -> x0, waiting for transfers between devices: 203 us -> none  [the longest x1 141 us: shards(): in_total = lax.psum(jnp.stack(in_grads).astype(f32), 'replica')]
    pallas_call x4 -> x6, Pallas kernels: 144 us -> 309 us  [the longest x4 210 us: grid_call(): pl.pallas_call(kernel, grid=grid, in_specs=in_specs + engine.in_specs(),...]
    reduce_scatter x4 -> x0, waiting for transfers between devices: 122 us -> none  [the longest x2 119 us: shards(): lax.psum_scatter(t_mm(normed, project_grad).astype(bf16), 'shard', scatte...]
    all_gather x4 -> x0, waiting for transfers between devices: 90.5 us -> none  [the longest x2 68.6 us: shards(): lax.all_gather(w_in[l], 'shard', axis=0, tiled=True)]
    psum x1 -> x0, blocking collectives: 39.4 us -> none  [shards(): lax.psum((jnp.stack(sums), jnp.stack(gain_grads)), ('replica', 'shard'))]
    convert_element_type x0 -> x2, local copies, waits for them, and re-layouts: none -> 15.8 us  [shards(): in_grad = t_mm(normed, project_grad).astype(bf16)]
    unnamed x56 -> x73, local copies, waits for them, and re-layouts: 13.9 us -> 4.54 us
  transfers between devices with their start and end apart: 10 -> 0, of which waited for: 8 -> 0; matrix products, arithmetic and copies ran while one was open for 14% -> 0% of each run, Pallas kernels for 9% -> 0%
where the time goes in v2:
time: 453 us; the launch traced here: 449 us
  Pallas kernels  309 us (68%)
  matrix products  88.8 us (20%)
  local copies, waits for them, and re-layouts  29.1 us (6%)
  other arithmetic  20.9 us (5%)
    pallas_call x4, Pallas kernels, grid_call(): pl.pallas_call(kernel, grid=grid, in_specs=in_specs + engine.in_specs(),...  210 us
    pallas_call x2, Pallas kernels, move(): pl.pallas_call(kernel, out_shape=engine.out_shapes(), in_specs=engine.in_...  99.6 us
    dot_general x4, matrix products, mm_t(): lax.dot_general(a, b, (((1,), (1,)), ((), ())), preferred_element_type=f32)  30.2 us
    dot_general x4, matrix products, mm(): return jnp.dot(a, b, preferred_element_type=f32)  29.7 us
    dot_general x4, matrix products, t_mm(): lax.dot_general(a, b, (((0,), (0,)), ((), ())), preferred_element_type=f32)  28.9 us
    convert_element_type x2, local copies, waits for them, and re-layouts, shards(): in_grad = t_mm(normed, project_grad).astype(bf16)  15.8 us

profile of v2, /device:TPU:0, one launch (start us, length us, event | category | flops | bytes accessed | tf_op | source)
XLA Modules:
  0.0 449.5 jit_solution(430570362750556543)
XLA Ops:
  0.7 0.9 fusion.18
  1.6 0.8 fusion.19
  6.1 1.9 fusion.3
  9.2 0.8 fusion.24
  12.0 1.0 and_convert_fusion.refs_9_
  13.8 0.9 slice_bitcast_fusion
  15.4 1.7 fusion.1
  17.1 37.9 %gather_first.1 = (bf16[768,3352]{1,0:T(8,128)(2,1)}, bf16[1536,768]{1,0:T(8,128)(2,1)}) custom-call(bf16[96,3352]{1,0:T(8,128)(2,1)} %get-tuple-element.101.refs_0_, bf16[192,768]{1,0:T(8,128)(2,1)} %get-tuple-element.103.refs_1_), custom_call_target="tpu_custom_call" | custom-call | tf_op jit(solution)/shard_map/gather_first/pallas_call | solution.py:647
  55.0 11.8 %fusion.25.refs_0_.refs_1_ = f32[1024,3352]{1,0:T(8,128)} fusion(bf16[1024,768]{1,0:T(8,128)(2,1)S(1)} %fusion.5, bf16[768,3352]{1,0:T(8,128)(2,1)} %get-tuple-element.42), kind=kOutput, calls=%fused_computation.103 | convolution fusion | flops 5272240128 | bytes 20451328 | tf_op jit(solution)/shard_map/dot_general | solution.py:32
  66.9 31.5 %mixer_forward_sending.2 = (bf16[1024,1536]{1,0:T(8,128)(2,1)S(1)}, f32[1024,1536]{1,0:T(8,128)}, bf16[1024,1536]{1,0:T(8,128)(2,1)}, bf16[768,3352]{1,0:T(8,128)(2,1)}) custom-call(f32[1024,3352]{1,0:T(8,128)} %fusion.25.refs_0_.refs_1_, f32[8,1792]{1,0:T(8,128)S(1)} %get-tuple-element.127.refs_1_.refs_5_, f32[8,128]{1,0:T(8,128)S(1)} %get-tuple-element.125.refs_2_.refs_6_, ...), custom_call_target="tpu_custom_call" | custom-call | tf_op jit(solution)/shard_map/mixer_forward_sending/pallas_call | solution.py:694
  98.5 2.8 multiply_reduce_fusion.2
  102.1 9.2 %fusion.20.refs_0_.refs_1_ = f32[1024,3352]{1,0:T(8,128)} fusion(bf16[768,3352]{1,0:T(8,128)(2,1)S(1)} %copy-done.28, f32[1024,768]{1,0:T(8,128)S(1)} %get-tuple-element.129, f32[768]{0:T(1024)S(1)} %get-tuple-element.98, f32[1024]{0:T(1024)S(1)} %add_rsqrt_fusion), kind=kOutput, calls=%fused_computation.98 | convolution fusion | flops 5274599424 | bytes 22031360 | tf_op jit(solution)/shard_map/dot_general | solution.py:32
  111.3 26.4 %mixer_forward_sending.3 = (bf16[1024,1536]{1,0:T(8,128)(2,1)}, f32[1024,1536]{1,0:T(8,128)}, bf16[1024,1536]{1,0:T(8,128)(2,1)}, bf16[1536,768]{1,0:T(8,128)(2,1)S(1)}) custom-call(f32[1024,3352]{1,0:T(8,128)} %fusion.20.refs_0_.refs_1_, f32[8,1792]{1,0:T(8,128)S(1)} %get-tuple-element.126.refs_1_.refs_5_, f32[8,128]{1,0:T(8,128)S(1)} %get-tuple-element.124.refs_2_.refs_6_, ...), custom_call_target="tpu_custom_call" | custom-call | tf_op jit(solution)/shard_map/mixer_forward_sending/pallas_call | solution.py:694
  137.8 5.8 %multiply_convert_fusion = bf16[1024,768]{1,0:T(8,128)(2,1)} fusion(f32[1024,768]{1,0:T(8,128)S(1)} %get-tuple-element.129, bf16[1024,1536]{1,0:T(8,128)(2,1)} %get-tuple-element.46, bf16[1536,768]{1,0:T(8,128)(2,1)S(1)} %get-tuple-element.47, f32[1024]{0:T(1024)S(1)} %bitcast.131), kind=kOutput, calls=%fused_computation.25 | convolution fusion | flops 2418278400 | bytes 10227712 | tf_op jit(solution)/shard_map/dot_general | solution.py:32
  143.6 4.0 convolution_convert_fusion.5.refs_10_
  147.5 4.0 convolution_convert_fusion.3.refs_4_
  151.6 58.2 %mixer_backward_sending.2 = (bf16[1024,3352]{1,0:T(8,128)(2,1)}, f32[8,1792]{1,0:T(8,128)}, f32[192,768]{1,0:T(8,128)}) custom-call(f32[1024,3352]{1,0:T(8,128)} %fusion.20.refs_0_.refs_1_, f32[1024,3352]{1,0:T(8,128)} %fusion.20.refs_0_.refs_1_, f32[1024,1536]{1,0:T(8,128)} %get-tuple-element.48.refs_2_, bf16[1024,1536]{1,0:T(8,128)(2,1)} %get-tuple-element.49.refs_3_, ...), custom_call_target="tpu_custom_call" | custom-call | tf_op jit(solution)/shard_map/mixer_backward_sending/pallas_call | solution.py:694
  209.8 10.9 %multiply_reduce_fusion = (f32[768]{0:T(1024)S(1)}, f32[1024]{0:T(1024)S(1)}, f32[1024,768]{1,0:T(8,128)S(1)}) fusion(f32[1024,768]{1,0:T(8,128)} %copy-done.12, f32[1024]{0:T(1024)S(1)} %add_rsqrt_fusion, f32[768]{0:T(1024)S(1)} %get-tuple-element.98, bf16[1024,3352]{1,0:T(8,128)(2,1)} %get-tuple-element.50, bf16[768,3352]{1,0:T(8,128)(2,1)} %get-tuple-element.45), kind=kOutput, calls=%fused_computation.23 | convolution fusion | flops 5276956672 | bytes 18319360 | tf_op jit(solution)/shard_map/dot_general | solution.py:36
  220.7 1.2 fusion.2
  222.6 4.0 convolution_convert_fusion.4.refs_11_
  226.5 4.2 convolution_convert_fusion.2.refs_4_
  230.7 10.3 %convolution_convert_fusion.1 = bf16[768,3352]{0,1:T(8,128)(2,1)} fusion(bf16[1024,3352]{1,0:T(8,128)(2,1)S(1)} %bitcast.139, f32[1024,768]{1,0:T(8,128)S(1)} %copy-done.13, f32[768]{0:T(1024)S(1)} %get-tuple-element.98, f32[1024]{0:T(1024)S(1)} %add_rsqrt_fusion), kind=kOutput, calls=%fused_computation.1 | convolution fusion | flops 5277173760 | bytes 15166464 | tf_op jit(solution)/shard_map/dot_general | solution.py:40
  241.0 7.9 %copy.54.refs_10_ = bf16[768,3352]{1,0:T(8,128)(2,1)} copy(bf16[768,3352]{0,1:T(8,128)(2,1)} %convolution_convert_fusion.1) | data formatting | bytes 10297344 | tf_op jit(solution)/shard_map/convert_element_type | solution.py:849
  248.9 93.6 %mixer_backward_sending.3 = (bf16[1024,3352]{1,0:T(8,128)(2,1)}, f32[8,1792]{1,0:T(8,128)}, f32[96,3352]{1,0:T(8,128)}, f32[192,768]{1,0:T(8,128)}) custom-call(f32[1024,3352]{1,0:T(8,128)} %fusion.25.refs_0_.refs_1_, f32[1024,3352]{1,0:T(8,128)} %fusion.25.refs_0_.refs_1_, f32[1024,1536]{1,0:T(8,128)} %get-tuple-element.51.refs_2_, ...), custom_call_target="tpu_custom_call" | custom-call | tf_op jit(solution)/shard_map/mixer_backward_sending/pallas_call | solution.py:694
  342.5 11.1 %fusion.9 = (f32[768]{0:T(1024)S(1)}, f32[1024]{0:T(1024)S(1)}, f32[1024,768]{1,0:T(8,128)}) fusion(bf16[2,1,512,768]{3,2,1,0:T(8,128)(2,1)S(1)} %copy-done.9, f32[1024]{0:T(1024)S(1)} %bitcast.125, f32[768]{0:T(1024)S(1)} %get-tuple-element.99, bf16[1024,3352]{1,0:T(8,128)(2,1)} %get-tuple-element.53, bf16[768,3352]{1,0:T(8,128)(2,1)} %get-tuple-element.42), kind=kOutput, calls=%fused_computation.22 | convolution fusion | flops 5277743104 | bytes 16746496 | tf_op jit(solution)/shard_map/dot_general | solution.py:36
  354.2 5.3 %fusion.7 = f32[1024,768]{1,0:T(8,128)} fusion(bf16[2,1,512,768]{3,2,1,0:T(8,128)(2,1)S(1)} %copy-done.9, f32[1024,768]{1,0:T(8,128)} %copy-done.10, f32[1024,768]{1,0:T(8,128)} %get-tuple-element.131, f32[1024]{0:T(1024)S(1)} %fusion.16, f32[768]{0:T(1024)S(1)} %get-tuple-element.99, f32[1024]{0:T(1024)S(1)} %bitcast.127), kind=kLoop, calls=%fused_computation.20 | loop fusion | flops 4718592 | bytes 11021312 | tf_op jit(solution)/shard_map/sub | solution.py:855
  359.5 1.1 pad_maximum_fusion.1
  360.6 0.8 copy-done.27
  361.4 10.7 %convolution_convert_fusion = bf16[768,3352]{0,1:T(8,128)(2,1)} fusion(bf16[1024,768]{1,0:T(8,128)(2,1)S(1)} %copy-done.15, bf16[1024,3352]{1,0:T(8,128)(2,1)S(1)} %copy-done.27), kind=kOutput, calls=%fused_computation | convolution fusion | flops 5274814464 | bytes 13586432 | tf_op jit(solution)/shard_map/dot_general | solution.py:40
  372.1 7.9 %copy.55.refs_0_ = bf16[768,3352]{1,0:T(8,128)(2,1)} copy(bf16[768,3352]{0,1:T(8,128)(2,1)} %convolution_convert_fusion) | data formatting | bytes 10297344 | tf_op jit(solution)/shard_map/convert_element_type | solution.py:849
  380.0 61.7 %reduce_last.1 = (f32[96,3352]{1,0:T(8,128)}, f32[16,1792]{1,0:T(8,128)}) custom-call(bf16[768,3352]{1,0:T(8,128)(2,1)} %copy.55.refs_0_, f32[16,1792]{1,0:T(8,128)} %bitcast.118), custom_call_target="tpu_custom_call" | custom-call | tf_op jit(solution)/shard_map/reduce_last/pallas_call | solution.py:647
  441.8 3.0 pad_maximum_fusion
  (128 shorter events, 14.6 us)
Async XLA Ops:
  0.6 12.4 %copy-start.19 = (bf16[2,192,768]{2,1,0:T(8,128)(2,1)S(1)}, bf16[2,192,768]{2,1,0:T(8,128)(2,1)}, u32[]{:S(2)}) copy-start(bf16[2,192,768]{2,1,0:T(8,128)(2,1)} %param.27) | copy-start | bytes 1769476
  6.1 8.7 %copy-start.9 = (bf16[2,1,512,768]{3,2,1,0:T(8,128)(2,1)S(1)}, bf16[2,1,512,768]{3,2,1,0:T(8,128)(2,1)}, u32[]{:S(2)}) copy-start(bf16[2,1,512,768]{3,2,1,0:T(8,128)(2,1)} %param.15) | copy-start | bytes 4718596
  8.1 58.8 %copy-start.5 = (f32[8,128]{1,0:T(8,128)}, f32[8,128]{1,0:T(8,128)S(1)}, u32[]{:S(2)}) copy-start(f32[8,128]{1,0:T(8,128)S(1)} %get-tuple-element.125.refs_2_.refs_6_) | copy-start | bytes 12292
  8.1 103.2 %copy-start.6 = (f32[8,128]{1,0:T(8,128)}, f32[8,128]{1,0:T(8,128)S(1)}, u32[]{:S(2)}) copy-start(f32[8,128]{1,0:T(8,128)S(1)} %get-tuple-element.124.refs_2_.refs_6_) | copy-start | bytes 12292
  9.2 4.6 %copy-start.17 = (bf16[2,96,3352]{2,1,0:T(8,128)(2,1)S(1)}, bf16[2,96,3352]{2,1,0:T(8,128)(2,1)}, u32[]{:S(2)}) copy-start(bf16[2,96,3352]{2,1,0:T(8,128)(2,1)} %param.20) | copy-start | bytes 3861508
  11.7 55.2 %copy-start.1 = (f32[8,1792]{1,0:T(8,128)}, f32[8,1792]{1,0:T(8,128)S(1)}, u32[]{:S(2)}) copy-start(f32[8,1792]{1,0:T(8,128)S(1)} %get-tuple-element.127.refs_1_.refs_5_) | copy-start | bytes 172036
  11.7 99.6 %copy-start.2 = (f32[8,1792]{1,0:T(8,128)}, f32[8,1792]{1,0:T(8,128)S(1)}, u32[]{:S(2)}) copy-start(f32[8,1792]{1,0:T(8,128)S(1)} %get-tuple-element.126.refs_1_.refs_5_) | copy-start | bytes 172036
  11.8 55.1 %copy-start.3 = (f32[8,1536]{1,0:T(8,128)}, f32[8,1536]{1,0:T(8,128)S(1)}, u32[]{:S(2)}) copy-start(f32[8,1536]{1,0:T(8,128)S(1)} %get-tuple-element.123.refs_3_.refs_7_) | copy-start | bytes 147460
  11.8 99.5 %copy-start.4 = (f32[8,1536]{1,0:T(8,128)}, f32[8,1536]{1,0:T(8,128)S(1)}, u32[]{:S(2)}) copy-start(f32[8,1536]{1,0:T(8,128)S(1)} %get-tuple-element.122.refs_3_.refs_7_) | copy-start | bytes 147460
  12.0 99.3 %copy-start = (bf16[128,1536]{1,0:T(8,128)(2,1)}, bf16[128,1536]{1,0:T(8,128)(2,1)S(1)}, u32[]{:S(2)}) copy-start(bf16[128,1536]{1,0:T(8,128)(2,1)S(1)} %and_convert_fusion.1.refs_4_.refs_8_) | copy-start | bytes 1179652
  15.4 39.6 %copy-start.14 = (bf16[1024,768]{1,0:T(8,128)(2,1)}, bf16[1024,768]{1,0:T(8,128)(2,1)S(1)}, u32[]{:S(2)}) copy-start(bf16[1024,768]{1,0:T(8,128)(2,1)S(1)} %fusion.5) | copy-start | bytes 4718596
  66.9 31.6 %copy-start.30 = (bf16[1536,768]{1,0:T(8,128)(2,1)S(1)}, bf16[1536,768]{1,0:T(8,128)(2,1)}, u32[]{:S(2)}) copy-start(bf16[1536,768]{1,0:T(8,128)(2,1)} %get-tuple-element.44) | copy-start | bytes 7077892
  98.4 2.9 copy-start.7
  98.5 3.6 copy-start.28
  101.3 36.4 %copy-start.12 = (f32[1024,768]{1,0:T(8,128)}, f32[1024,768]{1,0:T(8,128)S(1)}, u32[]{:S(2)}) copy-start(f32[1024,768]{1,0:T(8,128)S(1)} %get-tuple-element.129) | copy-start | bytes 9437188
  137.7 5.8 %copy-start.16 = (bf16[1024,768]{1,0:T(8,128)(2,1)S(1)}, bf16[1024,768]{1,0:T(8,128)(2,1)}, u32[]{:S(2)}) copy-start(bf16[1024,768]{1,0:T(8,128)(2,1)} %fusion.1) | copy-start | bytes 4718596
  137.7 5.8 %copy-start.29 = (bf16[1024,1536]{1,0:T(8,128)(2,1)S(1)}, bf16[1024,1536]{1,0:T(8,128)(2,1)}, u32[]{:S(2)}) copy-start(bf16[1024,1536]{1,0:T(8,128)(2,1)} %get-tuple-element.46) | copy-start | bytes 9437188
  209.7 10.9 %copy-start.13 = (f32[1024,768]{1,0:T(8,128)S(1)}, f32[1024,768]{1,0:T(8,128)}, u32[]{:S(2)}) copy-start(f32[1024,768]{1,0:T(8,128)} %copy-done.12) | copy-start | bytes 9437188
  222.6 4.0 copy-start.10
  222.6 4.0 copy-start.31
  222.6 8.1 %slice-start = ((s8[7077888]{0:T(1024)(128)(4,1)}), s8[4194304]{0:T(1024)(128)(4,1)S(1)}, s32[]{:S(2)}) async-start(s8[7077888]{0:T(1024)(128)(4,1)} %bitcast.138), calls=%async_computation | async-start | bytes 8388608
  226.5 4.2 slice-start.1
  342.5 11.2 %copy-start.24 = (f32[8,1792]{1,0:T(8,128)S(1)}, f32[8,1792]{1,0:T(8,128)}, u32[]{:S(2)}) copy-start(f32[8,1792]{1,0:T(8,128)} %get-tuple-element.55) | copy-start | bytes 172036
  342.5 11.2 %copy-start.25 = (f32[8,1792]{1,0:T(8,128)S(1)}, f32[8,1792]{1,0:T(8,128)}, u32[]{:S(2)}) copy-start(f32[8,1792]{1,0:T(8,128)} %get-tuple-element.54) | copy-start | bytes 172036
  354.1 5.4 %copy-start.22 = (f32[2,8,1792]{2,1,0:T(8,128)}, f32[2,8,1792]{2,1,0:T(8,128)S(1)}, u32[]{:S(2)}) copy-start(f32[2,8,1792]{2,1,0:T(8,128)S(1)} %scatter.4) | copy-start | bytes 344068
  354.1 5.4 %copy-start.20 = (f32[192,768]{1,0:T(8,128)S(1)}, f32[192,768]{1,0:T(8,128)}, u32[]{:S(2)}) copy-start(f32[192,768]{1,0:T(8,128)} %get-tuple-element.60) | copy-start | bytes 1769476
  354.1 5.4 %copy-start.21 = (f32[192,768]{1,0:T(8,128)S(1)}, f32[192,768]{1,0:T(8,128)}, u32[]{:S(2)}) copy-start(f32[192,768]{1,0:T(8,128)} %get-tuple-element.59) | copy-start | bytes 1769476
  354.1 6.5 %copy-start.15 = (bf16[1024,768]{1,0:T(8,128)(2,1)S(1)}, bf16[1024,768]{1,0:T(8,128)(2,1)}, u32[]{:S(2)}) copy-start(bf16[1024,768]{1,0:T(8,128)(2,1)} %copy-done.14) | copy-start | bytes 4718596
  354.2 7.3 %copy-start.27 = (bf16[1024,3352]{1,0:T(8,128)(2,1)S(1)}, bf16[1024,3352]{1,0:T(8,128)(2,1)}, u32[]{:S(2)}) copy-start(bf16[1024,3352]{1,0:T(8,128)(2,1)} %get-tuple-element.53) | copy-start | bytes 20594692
  380.0 61.7 %copy-start.18 = (f32[96,3352]{1,0:T(8,128)S(1)}, f32[96,3352]{1,0:T(8,128)}, u32[]{:S(2)}) copy-start(f32[96,3352]{1,0:T(8,128)} %get-tuple-element.58) | copy-start | bytes 3861508
  441.8 3.1 copy-start.23
  441.8 3.6 copy-start.26
  (2 other events, 3.5 us)
